TPU v7x, 512 devices: a whole 4x8x8 slice. The times are simulated.
512 devices in a mesh: grp: 8 (over y_lo, core), tile: 64 (over y_hi, x, z).
Axes of the slice: x: 4, y: 8 (y_hi: 2, y_lo: 4; y = y_hi * 4 + y_lo), z: 8, core: 2. Of those that a mesh axis runs over, the one named last changes fastest.
Arguments:
- hidden: bfloat16 [8, 512, 128, 128], P('grp', 'tile'), may hold values from -13 to 13
- cotangent: float32 [8, 512, 128], P('grp', 'tile'), may hold values from -16 to 16
- spectral_w: bfloat16 [4096, 256], P('tile'), may hold values from -0.375 to 0.375
- conv_k: float32 [9, 128], replicated, may hold values from -2 to 2
- proj_w: float32 [128], replicated, may hold values from -0.5 to 0.5
Outputs:
- grad_hidden: float32 [8, 512, 128, 128], P('grp', 'tile')
- grad_spectral: float32 [4096, 256], P('tile')
- grad_conv: float32 [9, 128], replicated
- grad_proj: float32 [128], replicated
All inputs are finite; a program needn't handle non-finite values.
Results may differ from a plain program's by a relative error of at most 0.015.
Values may be sent and summed in bfloat16 or wider, within the bound.
No kernel may reach another device: no remote copies, remote signals or barrier semaphores. Data moves between devices by JAX's collectives and lax.ppermute only.
A program may use at most 64 MiB of HBM per device.

v0:
```python
import jax
import jax.numpy as jnp
from jax import lax
from jax.sharding import PartitionSpec as P

HIGH = lax.Precision.HIGHEST


def padded(block, sides, width):
    for axis, dim in sides:
        count = lax.axis_size(axis)
        forward = [(i, i + 1) for i in range(count - 1)]
        backward = [(target, source) for source, target in forward]
        low = lax.ppermute(
            lax.slice_in_dim(block, block.shape[dim] - width, None, axis=dim), axis, forward
        )
        high = lax.ppermute(lax.slice_in_dim(block, 0, width, axis=dim), axis, backward)
        block = jnp.concatenate([low, block, high], axis=dim)
    return block


def spectral_tables(modes, bins):
    mode_idx = jnp.arange(modes, dtype=jnp.int32)
    bin_idx = jnp.arange(bins, dtype=jnp.int32)
    phase_int = mode_idx[:, None] * bin_idx[None, :] % bins
    angle_val = phase_int.astype(jnp.float32) * (2.0 * jnp.pi / bins)
    cosine = jnp.cos(angle_val)
    sine = jnp.sin(angle_val)
    forward_tab = jnp.concatenate([cosine, -sine], 0).astype(jnp.bfloat16)
    weight_k = jnp.where(mode_idx == 0, 1.0, 2.0).astype(jnp.float32)[:, None] / bins
    inverse_tab = jnp.concatenate([cosine * weight_k, -sine * weight_k], 0).T.astype(jnp.bfloat16)
    return (forward_tab, inverse_tab)


def build_mixer(weights, modes, chans):
    real_w = weights[:, :chans].reshape(modes, chans, chans)
    imag_w = weights[:, chans:].reshape(modes, chans, chans)
    upper = jnp.concatenate([real_w, imag_w], 2)
    lower = jnp.concatenate([-imag_w, real_w], 2)
    return jnp.concatenate([upper, lower], 1)


def gelu_pair(value):
    normal_cdf = 0.5 * (1.0 + jax.scipy.special.erf(value * 0.7071067811865476))
    return (
        value * normal_cdf,
        normal_cdf + value * jnp.exp(-0.5 * value * value) * 0.3989422804014327,
    )


def cell_backward(hidden_cells, local_term, cot_cells, mixer, forward_tab, inverse_tab, proj_w):
    modes = mixer.shape[0]
    chans = proj_w.shape[0]
    spec_h = jnp.einsum(
        "jb,pbc->jpc", forward_tab, hidden_cells, preferred_element_type=jnp.float32
    ).astype(jnp.bfloat16)
    h_cat = jnp.concatenate([spec_h[:modes], spec_h[modes:]], 2)
    mixed = jnp.einsum("kpa,kab->kpb", h_cat, mixer, preferred_element_type=jnp.float32).astype(
        jnp.bfloat16
    )
    mixed_stack = jnp.concatenate([mixed[:, :, :chans], mixed[:, :, chans:]], 0)
    spectral_out = jnp.einsum(
        "bj,jpo->pbo", inverse_tab, mixed_stack, preferred_element_type=jnp.float32
    )
    pre_act = spectral_out + local_term
    activ, slope = gelu_pair(pre_act)
    proj_grad = jnp.einsum("pb,pbo->o", cot_cells, activ, precision=HIGH)
    grad_pre = (cot_cells[:, :, None] * proj_w * slope).astype(jnp.bfloat16)
    grad_mix = jnp.einsum(
        "bj,pbo->jpo", inverse_tab, grad_pre, preferred_element_type=jnp.float32
    ).astype(jnp.bfloat16)
    grad_real = grad_mix[:modes]
    grad_imag = grad_mix[modes:]
    grad_cat = jnp.concatenate([grad_real, grad_imag], 2)
    grad_spec = jnp.einsum(
        "kpb,kab->kpa", grad_cat, mixer, preferred_element_type=jnp.float32
    ).astype(jnp.bfloat16)
    grad_stack = jnp.concatenate([grad_spec[:, :, :chans], grad_spec[:, :, chans:]], 0)
    grad_in = jnp.einsum("jb,jpc->pbc", forward_tab, grad_stack, preferred_element_type=jnp.float32)
    left_side = jnp.concatenate([spec_h[:modes], spec_h[modes:]], 1)
    right_side = jnp.concatenate([grad_cat, jnp.concatenate([grad_imag, -grad_real], 2)], 1)
    weight_term = jnp.einsum(
        "kpc,kpo->kco", left_side, right_side, preferred_element_type=jnp.float32
    ).reshape(modes * chans, 2 * chans)
    return (grad_pre, grad_in, weight_term, proj_grad)


def local(hidden, cotangent, spectral_w, conv_k, proj_w):
    rows_here, cols_here, bins_here, chans = hidden.shape
    modes = spectral_w.shape[0] * lax.axis_size("tile") // chans
    cell_count = rows_here * cols_here
    forward_tab, inverse_tab = spectral_tables(modes, bins_here)
    x_pad = padded(hidden, (("grp", 0), ("tile", 1)), 1)
    offsets = [(row_off, col_off) for row_off in (-1, 0, 1) for col_off in (-1, 0, 1)]
    local_term = jnp.zeros((rows_here, cols_here, bins_here, chans), jnp.float32)
    for index_d, (row_off, col_off) in enumerate(offsets):
        window = x_pad[1 + row_off : 1 + row_off + rows_here, 1 + col_off : 1 + col_off + cols_here]
        local_term = local_term + window.astype(jnp.float32) * conv_k[index_d]
    whole_w = lax.all_gather(spectral_w, "tile", axis=0, tiled=True)
    mixer = build_mixer(whole_w, modes, chans)
    grad_pre, grad_in, weight_term, proj_grad = cell_backward(
        hidden.reshape(cell_count, bins_here, chans),
        local_term.reshape(cell_count, bins_here, chans),
        cotangent.reshape(cell_count, bins_here),
        mixer,
        forward_tab,
        inverse_tab,
        proj_w,
    )
    grad_block = grad_pre.reshape(rows_here, cols_here, bins_here, chans)
    conv_part = jnp.stack(
        [
            jnp.einsum(
                "xybc,xybc->c",
                x_pad[1 + row_off : 1 + row_off + rows_here, 1 + col_off : 1 + col_off + cols_here],
                grad_block,
                preferred_element_type=jnp.float32,
            )
            for row_off, col_off in offsets
        ],
        0,
    )
    grad_pad = padded(grad_block, (("grp", 0), ("tile", 1)), 1)
    grad_hidden = grad_in.reshape(rows_here, cols_here, bins_here, chans)
    for index_d, (row_off, col_off) in enumerate(offsets):
        window = grad_pad[
            1 - row_off : 1 - row_off + rows_here, 1 - col_off : 1 - col_off + cols_here
        ]
        grad_hidden = grad_hidden + window.astype(jnp.float32) * conv_k[index_d]
    tile_share = lax.psum_scatter(weight_term, "tile", scatter_dimension=0, tiled=True)
    grad_spectral = lax.psum(tile_share.astype(jnp.bfloat16), "grp").astype(jnp.float32)
    conv_all, proj_all = lax.psum((conv_part, proj_grad), ("grp", "tile"))
    return (grad_hidden, grad_spectral, conv_all, proj_all)


def solution(mesh):
    in_specs = (P("grp", "tile", None, None), P("grp", "tile", None), P("tile", None), P(), P())
    out_specs = (P("grp", "tile", None, None), P("tile", None), P(), P())
    return jax.shard_map(local, mesh=mesh, in_specs=in_specs, out_specs=out_specs, check_vma=False)
```

profile of v0, /device:TPU:1, one launch (start us, length us, event | category | flops | bytes accessed | tf_op | source)
XLA Modules:
  0.0 639.4 jit_solution(11236863667525213482)
XLA Ops:
  7.9 1.1 copy.11
  9.1 8.8 %collective-permute-start.1 = (bf16[1,8,128,128]{2,3,1,0:T(8,128)(2,1)S(1)}, bf16[1,8,128,128]{2,3,1,0:T(8,128)(2,1)S(1)}, u32[]{:S(2)}, u32[]{:S(2)}) collective-permute-start(bf16[1,8,128,128]{2,3,1,0:T(8,128)(2,1)S(1)} %copy.11), channel_id=1, source_target_pairs={{64,0},{128,64},{192,128},{256,192},{320,256},{384,320},{448,384},... | collective-permute-start | bytes 786440 | tf_op jit(solution)/shard_map/ppermute | solution.py:17
  17.9 1.9 collective-permute-start
  19.9 1.1 convolution_convert_fusion.1
  21.1 1.0 slice_bitcast_fusion.8
  23.1 1.3 collective-permute-start.3
  24.4 4.0 collective-permute-start.2
  28.4 119.3 %all-gather.2.cloned.1.call-done = bf16[4096,256]{1,0:T(8,128)(2,1)} async-done(((bf16[64,256]{1,0:T(8,128)(2,1)}), bf16[4096,256]{1,0:T(8,128)(2,1)}) %all-gather.2.cloned.1.call-update) | async-done | bytes 2097168 | tf_op jit(solution)/shard_map/all_gather | solution.py:99
  147.7 1.7 fusion.52
  150.9 1.6 bitcast_convert_fusion
  152.8 2.7 fusion.24
  155.5 6.4 %collective-permute-start.5 = (bf16[1,8,128,128]{2,3,1,0:T(8,128)(2,1)S(1)}, bf16[1,8,128,128]{2,3,1,0:T(8,128)(2,1)}, u32[]{:S(2)}, u32[]{:S(2)}) collective-permute-start(bf16[1,8,128,128]{2,3,1,0:T(8,128)(2,1)S(1)} %bitcast.128), channel_id=1, source_target_pairs={{64,0},{128,64},{192,128},{256,192},{320,256},{384,320},{448,384},... | collective-permute-start | bytes 786440 | tf_op jit(solution)/shard_map/ppermute | solution.py:17
  161.9 5.1 collective-permute-start.4
  167.4 1.0 fusion.14
  168.4 1.2 fusion.15
  169.7 3.2 fusion.3
  173.5 97.4 %all-reduce = (f32[9,128]{1,0:T(8,128)}, f32[128]{0:T(128)}) all-reduce(f32[9,128]{1,0:T(8,128)S(1)} %stack.39, f32[128]{0:T(128)S(1)} %convolution_bitcast_fusion.2), channel_id=1, replica_groups=mesh['grp'=8,'tile'=64] {'grp','tile'}, use_global_device_ids=true, to_apply=%region_2.3 | all-reduce | flops 1280 | bytes 10240 | tf_op jit(solution)/shard_map/psum | solution.py:132
  271.8 1.3 collective-permute-start.6
  273.1 4.0 collective-permute-start.7
  277.5 1.3 collective-permute-done.7
  278.9 2.1 fusion.21
  281.1 1.0 copy.20
  282.1 273.8 %reduce-scatter.2.cloned.1.call-done = f32[64,256]{1,0:T(8,128)} async-done(((f32[4096,256]{1,0:T(8,128)}), f32[64,256]{1,0:T(8,128)}) %reduce-scatter.2.cloned.1.call-update) | async-done | bytes 65552 | tf_op jit(solution)/shard_map/reduce_scatter | solution.py:130
  556.7 75.3 %psum.21 = bf16[64,256]{1,0:T(8,128)(2,1)S(1)} all-reduce(bf16[64,256]{1,0:T(8,128)(2,1)S(1)} %convert_element_type.112), channel_id=1, replica_groups=mesh['grp'=8,'tile'=64] {'grp'}, use_global_device_ids=true, to_apply=%region_1.2 | all-reduce | flops 16384 | bytes 65536 | tf_op jit(solution)/shard_map/psum | solution.py:131
  (89 shorter events, 7.3 us)
Async XLA Ops:
  7.2 140.5 %all-gather.2.cloned.1.call-start = ((), (), s32[]{:S(2)}) async-start(), calls=%async_computation.1 | async-start | bytes 2129920 | tf_op jit(solution)/shard_map/all_gather | solution.py:99
  7.9 548.0 %reduce-scatter.2.cloned.1.call-start = ((), (), s32[]{:S(2)}) async-start(), calls=%async_computation.2 | async-start | bytes 4259840 | tf_op jit(solution)/shard_map/reduce_scatter | solution.py:130
  9.1 13.2 %collective-permute-start.1 = (bf16[1,8,128,128]{2,3,1,0:T(8,128)(2,1)S(1)}, bf16[1,8,128,128]{2,3,1,0:T(8,128)(2,1)S(1)}, u32[]{:S(2)}, u32[]{:S(2)}) collective-permute-start(bf16[1,8,128,128]{2,3,1,0:T(8,128)(2,1)S(1)} %copy.11), channel_id=1, source_target_pairs={{64,0},{128,64},{192,128},{256,192},{320,256},{384,320},{448,384},... | collective-permute-start | bytes 786440 | tf_op jit(solution)/shard_map/ppermute | solution.py:17
  17.9 5.2 collective-permute-start
  22.1 128.7 %copy-start.5 = (f32[128]{0:T(128)}, f32[128]{0:T(128)S(1)}, u32[]{:S(2)}) copy-start(f32[128]{0:T(128)S(1)} %get-tuple-element.35) | copy-start | bytes 1540
  22.1 128.7 %copy-start.7 = (f32[128]{0:T(128)}, f32[128]{0:T(128)S(1)}, u32[]{:S(2)}) copy-start(f32[128]{0:T(128)S(1)} %get-tuple-element.36) | copy-start | bytes 1540
  22.1 128.7 %copy-start.9 = (f32[128]{0:T(128)}, f32[128]{0:T(128)S(1)}, u32[]{:S(2)}) copy-start(f32[128]{0:T(128)S(1)} %get-tuple-element.37) | copy-start | bytes 1540
  22.1 128.7 %copy-start.11 = (f32[128]{0:T(128)}, f32[128]{0:T(128)S(1)}, u32[]{:S(2)}) copy-start(f32[128]{0:T(128)S(1)} %get-tuple-element.38) | copy-start | bytes 1540
  22.1 128.7 %copy-start.13 = (f32[128]{0:T(128)}, f32[128]{0:T(128)S(1)}, u32[]{:S(2)}) copy-start(f32[128]{0:T(128)S(1)} %get-tuple-element.39) | copy-start | bytes 1540
  22.1 128.7 %copy-start.15 = (f32[128]{0:T(128)}, f32[128]{0:T(128)S(1)}, u32[]{:S(2)}) copy-start(f32[128]{0:T(128)S(1)} %get-tuple-element.40) | copy-start | bytes 1540
  22.1 128.7 %copy-start.17 = (f32[128]{0:T(128)}, f32[128]{0:T(128)S(1)}, u32[]{:S(2)}) copy-start(f32[128]{0:T(128)S(1)} %get-tuple-element.41) | copy-start | bytes 1540
  22.1 128.7 %copy-start.19 = (f32[128]{0:T(128)}, f32[128]{0:T(128)S(1)}, u32[]{:S(2)}) copy-start(f32[128]{0:T(128)S(1)} %get-tuple-element.42) | copy-start | bytes 1540
  22.2 128.7 %copy-start.21 = (f32[128]{0:T(128)}, f32[128]{0:T(128)S(1)}, u32[]{:S(2)}) copy-start(f32[128]{0:T(128)S(1)} %get-tuple-element.43) | copy-start | bytes 1540
  23.1 127.7 %collective-permute-start.3 = (bf16[3,1,128,128]{2,3,1,0:T(8,128)(2,1)S(1)}, bf16[3,1,128,128]{2,3,1,0:T(8,128)(2,1)S(1)}, u32[]{:S(2)}, u32[]{:S(2)}) collective-permute-start(bf16[3,1,128,128]{2,3,1,0:T(8,128)(2,1)S(1)} %get-tuple-element.24), channel_id=1, source_target_pairs={{1,0},{2,1},{3,2},{4,3},{5,4},{6,5},{7,6},{8,7},{9,8},{10,9},{11,1... | collective-permute-start | bytes 294920 | tf_op jit(solution)/shard_map/ppermute | solution.py:17
  24.4 126.4 %collective-permute-start.2 = (bf16[3,1,128,128]{2,3,1,0:T(8,128)(2,1)S(1)}, bf16[3,1,128,128]{2,3,1,0:T(8,128)(2,1)S(1)}, u32[]{:S(2)}, u32[]{:S(2)}) collective-permute-start(bf16[3,1,128,128]{2,3,1,0:T(8,128)(2,1)S(1)} %get-tuple-element.25), channel_id=1, source_target_pairs={{0,1},{1,2},{2,3},{3,4},{4,5},{5,6},{6,7},{7,8},{8,9},{9,10},{10,1... | collective-permute-start | bytes 294920 | tf_op jit(solution)/shard_map/ppermute | solution.py:14
  155.5 115.4 %collective-permute-start.5 = (bf16[1,8,128,128]{2,3,1,0:T(8,128)(2,1)S(1)}, bf16[1,8,128,128]{2,3,1,0:T(8,128)(2,1)}, u32[]{:S(2)}, u32[]{:S(2)}) collective-permute-start(bf16[1,8,128,128]{2,3,1,0:T(8,128)(2,1)S(1)} %bitcast.128), channel_id=1, source_target_pairs={{64,0},{128,64},{192,128},{256,192},{320,256},{384,320},{448,384},... | collective-permute-start | bytes 786440 | tf_op jit(solution)/shard_map/ppermute | solution.py:17
  161.9 109.0 %collective-permute-start.4 = (bf16[1,8,128,128]{2,3,1,0:T(8,128)(2,1)S(1)}, bf16[1,8,128,128]{2,3,1,0:T(8,128)(2,1)}, u32[]{:S(2)}, u32[]{:S(2)}) collective-permute-start(bf16[1,8,128,128]{2,3,1,0:T(8,128)(2,1)S(1)} %bitcast.129), channel_id=1, source_target_pairs={{0,64},{64,128},{128,192},{192,256},{256,320},{320,384},{384,448},... | collective-permute-start | bytes 786440 | tf_op jit(solution)/shard_map/ppermute | solution.py:14
  169.6 109.2 %copy-start.6 = (f32[128]{0:T(128)S(1)}, f32[128]{0:T(128)}, u32[]{:S(2)}) copy-start(f32[128]{0:T(128)} %copy-done.5) | copy-start | bytes 1540
  169.6 109.2 %copy-start.8 = (f32[128]{0:T(128)S(1)}, f32[128]{0:T(128)}, u32[]{:S(2)}) copy-start(f32[128]{0:T(128)} %copy-done.7) | copy-start | bytes 1540
  169.6 109.2 %copy-start.10 = (f32[128]{0:T(128)S(1)}, f32[128]{0:T(128)}, u32[]{:S(2)}) copy-start(f32[128]{0:T(128)} %copy-done.9) | copy-start | bytes 1540
  169.6 109.2 %copy-start.12 = (f32[128]{0:T(128)S(1)}, f32[128]{0:T(128)}, u32[]{:S(2)}) copy-start(f32[128]{0:T(128)} %copy-done.11) | copy-start | bytes 1540
  169.7 109.2 %copy-start.14 = (f32[128]{0:T(128)S(1)}, f32[128]{0:T(128)}, u32[]{:S(2)}) copy-start(f32[128]{0:T(128)} %copy-done.13) | copy-start | bytes 1540
  271.8 5.8 collective-permute-start.6
  273.1 5.8 collective-permute-start.7
  (13 other events, 466.0 us)
Sparse Core Ops, SparseCore 0:
  12.6 135.0 all-gather.1
  155.6 400.1 reduce-scatter.1
where the time goes:
time: 640 us; the launch traced here: 639 us
  waiting for transfers between devices  396 us (62%)
  blocking collectives  173 us (27%)
  starting transfers between devices  32.8 us (5%)
  between operations  14.6 us (2%)
  matrix products  12.4 us (2%)
    reduce_scatter x1, waiting for transfers between devices, local(): lax.psum_scatter(weight_term, 'tile', scatter_dimension=0, tiled=True)  274 us
    all_gather x1, waiting for transfers between devices, local(): whole_w = lax.all_gather(spectral_w, 'tile', axis=0, tiled=True)  119 us
    psum x1, blocking collectives, local(): conv_all, proj_all = lax.psum((conv_part, proj_grad), ('grp', 'tile'))  97.4 us
    psum x1, blocking collectives, local(): lax.psum(tile_share.astype(jnp.bfloat16), 'grp').astype(jnp.float32)  75.3 us
    ppermute x4, starting transfers between devices, padded(): lax.ppermute(lax.slice_in_dim(block, 0, width, axis=dim), axis, backward)  17.8 us
    ppermute x4, starting transfers between devices, padded(): lax.ppermute(lax.slice_in_dim(block, block.shape[dim] - width, None, axis...  15 us
  transfers between devices with their start and end apart: 10, of which 5 were waited for; matrix products, arithmetic and copies ran while one was open for 3% of the time, Pallas kernels for 0%

commit v1 on v0

v1 whole, which is shorter than its diff:
```python
import jax
import jax.numpy as jnp
from jax import lax
from jax.sharding import PartitionSpec as P

BF = jnp.bfloat16
F32 = jnp.float32


def padded(block, axis, dim):
    count = lax.axis_size(axis)
    forward = [(i, i + 1) for i in range(count - 1)]
    backward = [(target, source) for source, target in forward]
    low = lax.ppermute(
        lax.slice_in_dim(block, block.shape[dim] - 1, None, axis=dim), axis, forward
    )
    high = lax.ppermute(lax.slice_in_dim(block, 0, 1, axis=dim), axis, backward)
    return low, high


def spectral_tables(modes, bins):
    mode_idx = jnp.arange(modes, dtype=jnp.int32)
    bin_idx = jnp.arange(bins, dtype=jnp.int32)
    phase_int = mode_idx[:, None] * bin_idx[None, :] % bins
    angle_val = phase_int.astype(F32) * (2.0 * jnp.pi / bins)
    cosine = jnp.cos(angle_val)
    sine = jnp.sin(angle_val)
    forward_tab = jnp.concatenate([cosine, -sine], 0).astype(BF)
    weight_k = jnp.where(mode_idx == 0, 1.0, 2.0).astype(F32)[:, None] / bins
    inverse_tab = jnp.concatenate([cosine * weight_k, -sine * weight_k], 0).T.astype(BF)
    return (forward_tab, inverse_tab)


def gelu_pair(value):
    normal_cdf = 0.5 * (1.0 + jax.scipy.special.erf(value * 0.7071067811865476))
    return (
        value * normal_cdf,
        normal_cdf + value * jnp.exp(-0.5 * value * value) * 0.3989422804014327,
    )


def split3(value):
    top = lax.reduce_precision(value, 8, 7)
    rest = value - top
    mid = lax.reduce_precision(rest, 8, 7)
    return jnp.stack([top, mid, rest - mid], 0).astype(BF)


def exchange(value, axis):
    return lax.all_to_all(value, axis, 0, 0, tiled=True)


def tied(*values):
    return lax.optimization_barrier(values)


def local(hidden, cotangent, spectral_w, conv_k, proj_w):
    rows_here, cols, bins, chans = hidden.shape
    groups = lax.axis_size("grp")
    tiles = lax.axis_size("tile")
    half = spectral_w.shape[0]
    modes = half * tiles // chans
    parts = chans // half
    cells = rows_here * cols
    forward_tab, inverse_tab = spectral_tables(modes, bins)
    real_w = spectral_w[:, :chans]
    imag_w = spectral_w[:, chans:]
    mixer = jnp.concatenate(
        [jnp.concatenate([real_w, imag_w], 1), jnp.concatenate([-imag_w, real_w], 1)], 0
    )
    block = hidden.reshape(cells, bins, chans)
    low_t, high_t = padded(hidden, "tile", 1)
    spec_h = jnp.einsum("jb,pbc->jpc", forward_tab, block, preferred_element_type=F32).astype(BF)
    sent = (
        spec_h.reshape(2, modes, cells, parts, half)
        .transpose(1, 3, 2, 0, 4)
        .reshape(tiles, cells, 2 * half)
    )
    got_h = exchange(sent, "tile")
    got_h, low_t, high_t = tied(got_h, low_t, high_t)
    wide = jnp.concatenate([low_t, hidden, high_t], 1)
    low_g, high_g = padded(wide, "grp", 0)
    own_h = got_h.reshape(tiles * cells, 2 * half)
    part = jnp.dot(own_h, mixer, preferred_element_type=F32).astype(BF)
    back = exchange(part.reshape(tiles, cells, 2 * chans), "tile")
    back, low_g, high_g, wide = tied(back, low_g, high_g, wide)
    x_pad = jnp.concatenate([low_g, wide, high_g], 0)
    inverse_twice = jnp.broadcast_to(
        inverse_tab.reshape(bins, 2, modes).transpose(0, 2, 1)[:, :, None, :],
        (bins, modes, parts, 2),
    )
    spectral_out = jnp.einsum(
        "bkhr,khpro->pbo",
        inverse_twice,
        back.reshape(modes, parts, cells, 2, chans),
        preferred_element_type=F32,
    )
    offsets = [(row_off, col_off) for row_off in (-1, 0, 1) for col_off in (-1, 0, 1)]
    local_term = jnp.zeros((rows_here, cols, bins, chans), F32)
    for index_d, (row_off, col_off) in enumerate(offsets):
        window = x_pad[1 + row_off : 1 + row_off + rows_here, 1 + col_off : 1 + col_off + cols]
        local_term = local_term + window.astype(F32) * conv_k[index_d]
    pre_act = spectral_out + local_term.reshape(cells, bins, chans)
    activ, slope = gelu_pair(pre_act)
    cot_cells = cotangent.reshape(cells, bins, 1)
    proj_part = jnp.sum(cot_cells * activ, (0, 1))
    grad_pre = (cot_cells * proj_w * slope).astype(BF)
    grad_block = grad_pre.reshape(rows_here, cols, bins, chans)
    low_gt, high_gt = padded(grad_block, "tile", 1)
    wide_grad = grad_block.astype(F32)
    sums = [
        jnp.sum(
            x_pad[
                1 + row_off : 1 + row_off + rows_here, 1 + col_off : 1 + col_off + cols
            ].astype(F32)
            * wide_grad,
            (0, 1, 2),
        )
        for row_off, col_off in offsets
    ] + [proj_part]
    count = len(sums)
    piece = count * chans // tiles
    small = split3(jnp.stack(sums, 0)).reshape(3, tiles, piece).transpose(1, 0, 2)
    small = jnp.pad(small.reshape(tiles, 3 * piece), ((0, 0), (0, chans - 3 * piece)))
    small = jnp.pad(small[:, None, :], ((0, 0), (0, cells - 1), (0, 0)))
    grad_mix = jnp.einsum("bj,pbo->jpo", inverse_tab, grad_pre, preferred_element_type=F32).astype(BF)
    grad_sent = grad_mix.reshape(2, modes, cells, chans).transpose(1, 2, 0, 3)
    grad_sent = jnp.broadcast_to(
        grad_sent.reshape(modes, 1, cells, 2 * chans), (modes, parts, cells, 2 * chans)
    )
    grad_sent = jnp.concatenate([grad_sent.reshape(tiles, cells, 2 * chans), small], 2)
    got_g = exchange(grad_sent, "tile")
    got_g, low_gt, high_gt = tied(got_g, low_gt, high_gt)
    grad_wide = jnp.concatenate([low_gt, grad_block, high_gt], 1)
    low_gg, high_gg = padded(grad_wide, "grp", 0)
    own_g = got_g[:, :, : 2 * chans].reshape(tiles * cells, 2 * chans)
    small_sum = jnp.sum(got_g[:, 0, 2 * chans : 2 * chans + 3 * piece].astype(F32), 0)
    small_sum = split3(small_sum.reshape(3, piece).sum(0)).reshape(1, 1, 3 * piece)
    small_sum = jnp.pad(small_sum, ((0, 0), (0, cells - 1), (0, 2 * half - 3 * piece)))
    small_sum = jnp.broadcast_to(small_sum, (tiles, cells, 2 * half))
    grad_spec = lax.dot_general(
        own_g, mixer, (((1,), (1,)), ((), ())), preferred_element_type=F32
    ).astype(BF)
    spec_sent = jnp.concatenate([grad_spec.reshape(tiles, cells, 2 * half), small_sum], 2)
    cross = lax.dot_general(own_h, own_g, (((0,), (0,)), ((), ())), preferred_element_type=F32)
    weight_part = jnp.concatenate(
        [
            cross[:half, :chans] + cross[half:, chans:],
            cross[:half, chans:] - cross[half:, :chans],
        ],
        1,
    ).astype(BF)
    got_s = exchange(spec_sent, "tile")
    got_s, low_gg, high_gg, weight_part = tied(got_s, low_gg, high_gg, weight_part)
    totals = got_s[:, 0, 2 * half : 2 * half + 3 * piece].reshape(tiles, 3, piece)
    totals = totals.transpose(1, 0, 2).reshape(3 * count * chans // (2 * chans), 2 * chans)
    last = jnp.concatenate([weight_part, totals], 0)
    last = exchange(jnp.broadcast_to(last, (groups,) + last.shape), "grp")
    grad_spectral = jnp.sum(last[:, :half].astype(F32), 0)
    totals = last[:, half:].astype(F32).reshape(groups, 3, count, chans)
    totals = jnp.sum(totals, (0, 1))
    grad_stack = (
        got_s[:, :, : 2 * half]
        .reshape(modes, parts, cells, 2, half)
        .transpose(3, 0, 2, 1, 4)
        .reshape(2 * modes, cells, chans)
    )
    grad_in = jnp.einsum("jb,jpc->pbc", forward_tab, grad_stack, preferred_element_type=F32)
    grad_pad = jnp.concatenate([low_gg, grad_wide, high_gg], 0)
    grad_hidden = grad_in.reshape(rows_here, cols, bins, chans)
    for index_d, (row_off, col_off) in enumerate(offsets):
        window = grad_pad[1 - row_off : 1 - row_off + rows_here, 1 - col_off : 1 - col_off + cols]
        grad_hidden = grad_hidden + window.astype(F32) * conv_k[index_d]
    return (grad_hidden, grad_spectral, totals[: count - 1], totals[count - 1])


def solution(mesh):
    in_specs = (P("grp", "tile", None, None), P("grp", "tile", None), P("tile", None), P(), P())
    out_specs = (P("grp", "tile", None, None), P("tile", None), P(), P())
    return jax.shard_map(local, mesh=mesh, in_specs=in_specs, out_specs=out_specs, check_vma=False)
```

time: 640 us -> 146 us (0.23)
  waiting for transfers between devices: 396 us -> 41.7 us
  blocking collectives: 173 us -> 0 us
  starting transfers between devices: 32.8 us -> 87.9 us
  between operations: 14.6 us -> 1.05 us
  matrix products: 12.4 us -> 5.2 us
    reduce_scatter x1 -> x0, waiting for transfers between devices: 274 us -> none  [local(): lax.psum_scatter(weight_term, 'tile', scatter_dimension=0, tiled=True)]
    psum x2 -> x0, blocking collectives: 173 us -> none  [the longest x1 97.4 us: local(): conv_all, proj_all = lax.psum((conv_part, proj_grad), ('grp', 'tile'))]
    all_gather x1 -> x0, waiting for transfers between devices: 119 us -> none  [local(): whole_w = lax.all_gather(spectral_w, 'tile', axis=0, tiled=True)]
    all_to_all x0 -> x5, starting transfers between devices: none -> 59.1 us  [exchange(): return lax.all_to_all(value, axis, 0, 0, tiled=True)]
    all_to_all x0 -> x5, waiting for transfers between devices: none -> 30.4 us  [exchange(): return lax.all_to_all(value, axis, 0, 0, tiled=True)]
    ppermute x8, waiting for transfers between devices: 2.6 us -> 11.3 us  [the longest x4 9.34 us: padded(): high = lax.ppermute(lax.slice_in_dim(block, 0, 1, axis=dim), axis, backward)]
    dot_general x8 -> x7, matrix products: 12.4 us -> 5.2 us  [the longest x1 1.37 us: local(): jnp.einsum('jb,jpc->pbc', forward_tab, grad_stack, preferred_element_type...]
  transfers between devices with their start and end apart: 10 -> 13, of which waited for: 5 -> 11; matrix products, arithmetic and copies ran while one was open for 3% -> 3% of each run, Pallas kernels for 0% -> 0%
where the time goes in v1:
time: 146 us; the launch traced here: 145 us
  starting transfers between devices  87.9 us (60%)
  waiting for transfers between devices  41.7 us (29%)
  local copies, waits for them, and re-layouts  6.51 us (4%)
  matrix products  5.2 us (4%)
  other arithmetic  2.92 us (2%)
    all_to_all x5, starting transfers between devices, exchange(): return lax.all_to_all(value, axis, 0, 0, tiled=True)  59.1 us
    all_to_all x5, waiting for transfers between devices, exchange(): return lax.all_to_all(value, axis, 0, 0, tiled=True)  30.4 us
    ppermute x4, starting transfers between devices, padded(): lax.ppermute(lax.slice_in_dim(block, block.shape[dim] - 1, None, axis=dim...  19.8 us
    ppermute x4, waiting for transfers between devices, padded(): high = lax.ppermute(lax.slice_in_dim(block, 0, 1, axis=dim), axis, backward)  9.34 us
    ppermute x4, starting transfers between devices, padded(): high = lax.ppermute(lax.slice_in_dim(block, 0, 1, axis=dim), axis, backward)  9.03 us
  transfers between devices with their start and end apart: 13, of which 11 were waited for; matrix products, arithmetic and copies ran while one was open for 3% of the time, Pallas kernels for 0%

profile of v1, /device:TPU:1, one launch (start us, length us, event | category | flops | bytes accessed | tf_op | source)
XLA Modules:
  0.0 145.3 jit_solution(6865904608652353643)
XLA Ops:
  1.4 1.3 collective-permute-start.1
  2.7 5.5 %collective-permute-start = (bf16[1,1,128,128]{3,2,1,0:T(8,128)(2,1)S(1)}, bf16[1,1,128,128]{3,2,1,0:T(8,128)(2,1)S(1)}, u32[]{:S(2)}, u32[]{:S(2)}) collective-permute-start(bf16[1,1,128,128]{3,2,1,0:T(8,128)(2,1)S(1)} %get-tuple-element.51), channel_id=1, source_target_pairs={{0,1},{1,2},{2,3},{3,4},{4,5},{5,6},{6,7},{7,8},{8,9},{9,10},{10,1... | collective-permute-start | bytes 98312 | tf_op jit(solution)/shard_map/ppermute | solution.py:14
  8.3 1.1 convolution_convert_fusion.3
  10.6 20.9 %all-to-all-start = ((bf16[64,8,128]{2,1,0:T(8,128)(2,1)}), bf16[64,8,128]{2,1,0:T(8,128)(2,1)S(1)}, u32[]{:S(2)}, u32[]{:S(2)}) async-start(bf16[64,8,128]{2,1,0:T(8,128)(2,1)} %reshape.383), calls=%async_computation | async-start | bytes 262144 | tf_op jit(solution)/shard_map/all_to_all | solution.py:50
  31.6 13.5 %all-to-all-done = bf16[64,8,128]{2,1,0:T(8,128)(2,1)S(1)} async-done(((bf16[64,8,128]{2,1,0:T(8,128)(2,1)}), bf16[64,8,128]{2,1,0:T(8,128)(2,1)S(1)}, u32[]{:S(2)}, u32[]{:S(2)}) %all-to-all-start) | async-done | bytes 131104 | tf_op jit(solution)/shard_map/all_to_all | solution.py:50
  45.1 0.9 fusion.10
  46.0 4.8 %all-to-all-start.1 = ((bf16[64,8,256]{2,1,0:T(8,128)(2,1)}), bf16[64,8,256]{2,1,0:T(8,128)(2,1)S(1)}, u32[]{:S(2)}, u32[]{:S(2)}) async-start(bf16[64,8,256]{2,1,0:T(8,128)(2,1)} %fusion.10), calls=%async_computation.1 | async-start | bytes 524288 | tf_op jit(solution)/shard_map/all_to_all | solution.py:50
  50.9 4.5 %collective-permute-start.3 = (bf16[1,10,128,128]{3,2,1,0:T(8,128)(2,1)S(1)}, bf16[1,10,128,128]{3,2,1,0:T(8,128)(2,1)S(1)}, u32[]{:S(2)}, u32[]{:S(2)}) collective-permute-start(bf16[1,10,128,128]{3,2,1,0:T(8,128)(2,1)S(1)} %constant_dynamic-update-slice_fusion), channel_id=1, source_target_pairs={{64,0},{128,64},{192,128},{256,192},{320,256},{384,320},{448,384},... | collective-permute-start | bytes 983048 | tf_op jit(solution)/shard_map/ppermute | solution.py:17
  55.4 3.7 %collective-permute-start.2 = (bf16[1,10,128,128]{3,2,1,0:T(8,128)(2,1)S(1)}, bf16[1,10,128,128]{3,2,1,0:T(8,128)(2,1)S(1)}, u32[]{:S(2)}, u32[]{:S(2)}) collective-permute-start(bf16[1,10,128,128]{3,2,1,0:T(8,128)(2,1)S(1)} %constant_dynamic-update-slice_fusion), channel_id=1, source_target_pairs={{0,64},{64,128},{128,192},{192,256},{256,320},{320,384},{384,448},... | collective-permute-start | bytes 983048 | tf_op jit(solution)/shard_map/ppermute | solution.py:14
  59.8 3.7 %collective-permute-done.3 = bf16[1,10,128,128]{3,2,1,0:T(8,128)(2,1)S(1)} collective-permute-done((bf16[1,10,128,128]{3,2,1,0:T(8,128)(2,1)S(1)}, bf16[1,10,128,128]{3,2,1,0:T(8,128)(2,1)S(1)}, u32[]{:S(2)}, u32[]{:S(2)}) %collective-permute-start.3) | collective-permute-done | bytes 327712 | tf_op jit(solution)/shard_map/ppermute | solution.py:17
  65.7 1.2 fusion.39
  68.8 13.1 %all-to-all-start.2 = ((bf16[64,8,384]{2,1,0:T(8,128)(2,1)}), bf16[64,8,384]{2,1,0:T(8,128)(2,1)S(1)}, u32[]{:S(2)}, u32[]{:S(2)}) async-start(bf16[64,8,384]{2,1,0:T(8,128)(2,1)} %fusion.47), calls=%async_computation.2 | async-start | bytes 786432 | tf_op jit(solution)/shard_map/all_to_all | solution.py:50
  81.9 1.3 collective-permute-start.5
  83.2 4.0 %collective-permute-start.4 = (bf16[1,1,128,128]{3,2,1,0:T(8,128)(2,1)S(1)}, bf16[1,1,128,128]{3,2,1,0:T(8,128)(2,1)S(1)}, u32[]{:S(2)}, u32[]{:S(2)}) collective-permute-start(bf16[1,1,128,128]{3,2,1,0:T(8,128)(2,1)S(1)} %get-tuple-element.49), channel_id=1, source_target_pairs={{0,1},{1,2},{2,3},{3,4},{4,5},{5,6},{6,7},{7,8},{8,9},{9,10},{10,1... | collective-permute-start | bytes 98312 | tf_op jit(solution)/shard_map/ppermute | solution.py:14
  87.2 1.5 %collective-permute-done.5 = bf16[1,1,128,128]{3,2,1,0:T(8,128)(2,1)S(1)} collective-permute-done((bf16[1,1,128,128]{3,2,1,0:T(8,128)(2,1)S(1)}, bf16[1,1,128,128]{3,2,1,0:T(8,128)(2,1)S(1)}, u32[]{:S(2)}, u32[]{:S(2)}) %collective-permute-start.5) | collective-permute-done | bytes 32800 | tf_op jit(solution)/shard_map/ppermute | solution.py:17
  88.8 8.0 %all-to-all-done.2 = bf16[64,8,384]{2,1,0:T(8,128)(2,1)S(1)} async-done(((bf16[64,8,384]{2,1,0:T(8,128)(2,1)}), bf16[64,8,384]{2,1,0:T(8,128)(2,1)S(1)}, u32[]{:S(2)}, u32[]{:S(2)}) %all-to-all-start.2) | async-done | bytes 393248 | tf_op jit(solution)/shard_map/all_to_all | solution.py:50
  98.1 11.6 %all-to-all-start.3 = ((bf16[64,8,256]{2,1,0:T(8,128)(2,1)}), bf16[64,8,256]{2,1,0:T(8,128)(2,1)S(1)}, u32[]{:S(2)}, u32[]{:S(2)}) async-start(bf16[64,8,256]{2,1,0:T(8,128)(2,1)} %pad_maximum_fusion.3), calls=%async_computation.3 | async-start | bytes 524288 | tf_op jit(solution)/shard_map/all_to_all | solution.py:50
  109.8 1.9 %collective-permute-start.7 = (bf16[1,10,128,128]{3,2,1,0:T(8,128)(2,1)S(1)}, bf16[1,10,128,128]{3,2,1,0:T(8,128)(2,1)S(1)}, u32[]{:S(2)}, u32[]{:S(2)}) collective-permute-start(bf16[1,10,128,128]{3,2,1,0:T(8,128)(2,1)S(1)} %pad_maximum_fusion), channel_id=1, source_target_pairs={{64,0},{128,64},{192,128},{256,192},{320,256},{384,320},{448,384},... | collective-permute-start | bytes 983048 | tf_op jit(solution)/shard_map/ppermute | solution.py:17
  111.7 6.7 %collective-permute-start.6 = (bf16[1,10,128,128]{3,2,1,0:T(8,128)(2,1)S(1)}, bf16[1,10,128,128]{3,2,1,0:T(8,128)(2,1)S(1)}, u32[]{:S(2)}, u32[]{:S(2)}) collective-permute-start(bf16[1,10,128,128]{3,2,1,0:T(8,128)(2,1)S(1)} %pad_maximum_fusion), channel_id=1, source_target_pairs={{0,64},{64,128},{128,192},{192,256},{256,320},{320,384},{384,448},... | collective-permute-start | bytes 983048 | tf_op jit(solution)/shard_map/ppermute | solution.py:14
  118.6 4.1 %collective-permute-done.7 = bf16[1,10,128,128]{3,2,1,0:T(8,128)(2,1)S(1)} collective-permute-done((bf16[1,10,128,128]{3,2,1,0:T(8,128)(2,1)S(1)}, bf16[1,10,128,128]{3,2,1,0:T(8,128)(2,1)S(1)}, u32[]{:S(2)}, u32[]{:S(2)}) %collective-permute-start.7) | collective-permute-done | bytes 327712 | tf_op jit(solution)/shard_map/ppermute | solution.py:17
  122.8 0.9 collective-permute-done.6
  125.2 8.7 %all-to-all-start.4 = ((bf16[8,79,256]{2,1,0:T(8,128)(2,1)}), bf16[8,79,256]{2,1,0:T(8,128)(2,1)S(1)}, u32[]{:S(2)}, u32[]{:S(2)}) async-start(bf16[8,79,256]{2,1,0:T(8,128)(2,1)} %broadcast_in_dim.46), calls=%async_computation.4 | async-start | bytes 655360 | tf_op jit(solution)/shard_map/all_to_all | solution.py:50
  134.6 1.4 fusion.9
  135.9 8.1 %all-to-all-done.4 = bf16[8,79,256]{2,1,0:T(8,128)(2,1)S(1)} async-done(((bf16[8,79,256]{2,1,0:T(8,128)(2,1)}), bf16[8,79,256]{2,1,0:T(8,128)(2,1)S(1)}, u32[]{:S(2)}, u32[]{:S(2)}) %all-to-all-start.4) | async-done | bytes 323616 | tf_op jit(solution)/shard_map/all_to_all | solution.py:50
  (78 shorter events, 12.0 us)
Async XLA Ops:
  1.4 30.2 %collective-permute-start.1 = (bf16[1,1,128,128]{3,2,1,0:T(8,128)(2,1)S(1)}, bf16[1,1,128,128]{3,2,1,0:T(8,128)(2,1)S(1)}, u32[]{:S(2)}, u32[]{:S(2)}) collective-permute-start(bf16[1,1,128,128]{3,2,1,0:T(8,128)(2,1)S(1)} %get-tuple-element.50), channel_id=1, source_target_pairs={{1,0},{2,1},{3,2},{4,3},{5,4},{6,5},{7,6},{8,7},{9,8},{10,9},{11,1... | collective-permute-start | bytes 98312 | tf_op jit(solution)/shard_map/ppermute | solution.py:17
  2.7 28.9 %collective-permute-start = (bf16[1,1,128,128]{3,2,1,0:T(8,128)(2,1)S(1)}, bf16[1,1,128,128]{3,2,1,0:T(8,128)(2,1)S(1)}, u32[]{:S(2)}, u32[]{:S(2)}) collective-permute-start(bf16[1,1,128,128]{3,2,1,0:T(8,128)(2,1)S(1)} %get-tuple-element.51), channel_id=1, source_target_pairs={{0,1},{1,2},{2,3},{3,4},{4,5},{5,6},{6,7},{7,8},{8,9},{9,10},{10,1... | collective-permute-start | bytes 98312 | tf_op jit(solution)/shard_map/ppermute | solution.py:14
  10.6 20.9 %copy-start.1 = (bf16[64,256]{1,0:T(8,128)(2,1)S(1)}, bf16[64,256]{1,0:T(8,128)(2,1)}, u32[]{:S(2)}) copy-start(bf16[64,256]{1,0:T(8,128)(2,1)} %param.7) | copy-start | bytes 98308
  10.6 34.5 %all-to-all-start = ((bf16[64,8,128]{2,1,0:T(8,128)(2,1)}), bf16[64,8,128]{2,1,0:T(8,128)(2,1)S(1)}, u32[]{:S(2)}, u32[]{:S(2)}) async-start(bf16[64,8,128]{2,1,0:T(8,128)(2,1)} %reshape.383), calls=%async_computation | async-start | bytes 262144 | tf_op jit(solution)/shard_map/all_to_all | solution.py:50
  46.0 4.8 %copy-start = (bf16[1,8,128,128]{3,2,1,0:T(8,128)(2,1)S(1)}, bf16[1,8,128,128]{3,2,1,0:T(8,128)(2,1)}, u32[]{:S(2)}) copy-start(bf16[1,8,128,128]{3,2,1,0:T(8,128)(2,1)} %param.5) | copy-start | bytes 786436
  46.0 18.9 %all-to-all-start.1 = ((bf16[64,8,256]{2,1,0:T(8,128)(2,1)}), bf16[64,8,256]{2,1,0:T(8,128)(2,1)S(1)}, u32[]{:S(2)}, u32[]{:S(2)}) async-start(bf16[64,8,256]{2,1,0:T(8,128)(2,1)} %fusion.10), calls=%async_computation.1 | async-start | bytes 524288 | tf_op jit(solution)/shard_map/all_to_all | solution.py:50
  50.9 12.7 %collective-permute-start.3 = (bf16[1,10,128,128]{3,2,1,0:T(8,128)(2,1)S(1)}, bf16[1,10,128,128]{3,2,1,0:T(8,128)(2,1)S(1)}, u32[]{:S(2)}, u32[]{:S(2)}) collective-permute-start(bf16[1,10,128,128]{3,2,1,0:T(8,128)(2,1)S(1)} %constant_dynamic-update-slice_fusion), channel_id=1, source_target_pairs={{64,0},{128,64},{192,128},{256,192},{320,256},{384,320},{448,384},... | collective-permute-start | bytes 983048 | tf_op jit(solution)/shard_map/ppermute | solution.py:17
  55.4 9.0 %collective-permute-start.2 = (bf16[1,10,128,128]{3,2,1,0:T(8,128)(2,1)S(1)}, bf16[1,10,128,128]{3,2,1,0:T(8,128)(2,1)S(1)}, u32[]{:S(2)}, u32[]{:S(2)}) collective-permute-start(bf16[1,10,128,128]{3,2,1,0:T(8,128)(2,1)S(1)} %constant_dynamic-update-slice_fusion), channel_id=1, source_target_pairs={{0,64},{64,128},{128,192},{192,256},{256,320},{320,384},{384,448},... | collective-permute-start | bytes 983048 | tf_op jit(solution)/shard_map/ppermute | solution.py:14
  59.1 0.7 copy-start.4
  65.0 0.7 copy-start.3
  65.0 0.7 copy-start.5
  68.8 28.0 %all-to-all-start.2 = ((bf16[64,8,384]{2,1,0:T(8,128)(2,1)}), bf16[64,8,384]{2,1,0:T(8,128)(2,1)S(1)}, u32[]{:S(2)}, u32[]{:S(2)}) async-start(bf16[64,8,384]{2,1,0:T(8,128)(2,1)} %fusion.47), calls=%async_computation.2 | async-start | bytes 786432 | tf_op jit(solution)/shard_map/all_to_all | solution.py:50
  81.9 6.8 %collective-permute-start.5 = (bf16[1,1,128,128]{3,2,1,0:T(8,128)(2,1)S(1)}, bf16[1,1,128,128]{3,2,1,0:T(8,128)(2,1)S(1)}, u32[]{:S(2)}, u32[]{:S(2)}) collective-permute-start(bf16[1,1,128,128]{3,2,1,0:T(8,128)(2,1)S(1)} %get-tuple-element.48), channel_id=1, source_target_pairs={{1,0},{2,1},{3,2},{4,3},{5,4},{6,5},{7,6},{8,7},{9,8},{10,9},{11,1... | collective-permute-start | bytes 98312 | tf_op jit(solution)/shard_map/ppermute | solution.py:17
  83.2 5.6 %collective-permute-start.4 = (bf16[1,1,128,128]{3,2,1,0:T(8,128)(2,1)S(1)}, bf16[1,1,128,128]{3,2,1,0:T(8,128)(2,1)S(1)}, u32[]{:S(2)}, u32[]{:S(2)}) collective-permute-start(bf16[1,1,128,128]{3,2,1,0:T(8,128)(2,1)S(1)} %get-tuple-element.49), channel_id=1, source_target_pairs={{0,1},{1,2},{2,3},{3,4},{4,5},{5,6},{6,7},{7,8},{8,9},{9,10},{10,1... | collective-permute-start | bytes 98312 | tf_op jit(solution)/shard_map/ppermute | solution.py:14
  98.1 26.0 %all-to-all-start.3 = ((bf16[64,8,256]{2,1,0:T(8,128)(2,1)}), bf16[64,8,256]{2,1,0:T(8,128)(2,1)S(1)}, u32[]{:S(2)}, u32[]{:S(2)}) async-start(bf16[64,8,256]{2,1,0:T(8,128)(2,1)} %pad_maximum_fusion.3), calls=%async_computation.3 | async-start | bytes 524288 | tf_op jit(solution)/shard_map/all_to_all | solution.py:50
  109.8 13.0 %collective-permute-start.7 = (bf16[1,10,128,128]{3,2,1,0:T(8,128)(2,1)S(1)}, bf16[1,10,128,128]{3,2,1,0:T(8,128)(2,1)S(1)}, u32[]{:S(2)}, u32[]{:S(2)}) collective-permute-start(bf16[1,10,128,128]{3,2,1,0:T(8,128)(2,1)S(1)} %pad_maximum_fusion), channel_id=1, source_target_pairs={{64,0},{128,64},{192,128},{256,192},{320,256},{384,320},{448,384},... | collective-permute-start | bytes 983048 | tf_op jit(solution)/shard_map/ppermute | solution.py:17
  111.7 12.0 %collective-permute-start.6 = (bf16[1,10,128,128]{3,2,1,0:T(8,128)(2,1)S(1)}, bf16[1,10,128,128]{3,2,1,0:T(8,128)(2,1)S(1)}, u32[]{:S(2)}, u32[]{:S(2)}) collective-permute-start(bf16[1,10,128,128]{3,2,1,0:T(8,128)(2,1)S(1)} %pad_maximum_fusion), channel_id=1, source_target_pairs={{0,64},{64,128},{128,192},{192,256},{256,320},{320,384},{384,448},... | collective-permute-start | bytes 983048 | tf_op jit(solution)/shard_map/ppermute | solution.py:14
  125.2 18.8 %all-to-all-start.4 = ((bf16[8,79,256]{2,1,0:T(8,128)(2,1)}), bf16[8,79,256]{2,1,0:T(8,128)(2,1)S(1)}, u32[]{:S(2)}, u32[]{:S(2)}) async-start(bf16[8,79,256]{2,1,0:T(8,128)(2,1)} %broadcast_in_dim.46), calls=%async_computation.4 | async-start | bytes 655360 | tf_op jit(solution)/shard_map/all_to_all | solution.py:50
  144.1 1.2 copy-start.2

commit v2 on v1

v2 whole, which is shorter than its diff:
```python
import jax
import jax.numpy as jnp
import numpy as np
from jax import lax
from jax.experimental import pallas as pl
from jax.experimental.pallas import tpu as pltpu
from jax.sharding import PartitionSpec as P

BF = jnp.bfloat16
F32 = jnp.float32


def shifted(block, axis, step):
    count = lax.axis_size(axis)
    pairs = [(i, i + step) for i in range(count) if 0 <= i + step < count]
    return lax.ppermute(block, axis, pairs)


def edge_pack(columns, cot):
    flat = columns.reshape(-1, columns.shape[-1])
    return jnp.concatenate([flat, cot, jnp.zeros((5, flat.shape[1]), BF)], 0)


def edge_unpack(packed, bins):
    columns = packed[: 2 * bins].reshape(2, bins, -1)
    cot = packed[2 * bins : 2 * bins + 3].astype(F32).sum(0)
    return columns, cot[None]


def to_spec(forward_tab, block):
    spec = jnp.einsum("jb,pbc->jpc", forward_tab, block, preferred_element_type=F32)
    return spec.astype(BF)


def spectral_tables(modes, bins):
    phase_int = np.arange(modes)[:, None] * np.arange(bins)[None, :] % bins
    angle_val = phase_int.astype(np.float32) * np.float32(2.0 * np.pi / bins)
    cosine = np.cos(angle_val)
    sine = np.sin(angle_val)
    forward_tab = np.concatenate([cosine, -sine], 0)
    weight_k = np.where(np.arange(modes) == 0, 1.0, 2.0).astype(np.float32)[:, None] / bins
    inverse_tab = np.concatenate([cosine * weight_k, -sine * weight_k], 0).T
    tables = np.concatenate([forward_tab, inverse_tab.T], 0)
    return jnp.asarray(tables.astype(jnp.bfloat16))


def gelu_pair(value):
    normal_cdf = 0.5 * (1.0 + jax.scipy.special.erf(value * 0.7071067811865476))
    return (
        value * normal_cdf,
        normal_cdf + value * jnp.exp(-0.5 * value * value) * 0.3989422804014327,
    )


def split3(value):
    top = lax.reduce_precision(value, 8, 7)
    rest = value - top
    mid = lax.reduce_precision(rest, 8, 7)
    return jnp.stack([top, mid, rest - mid], 0).astype(BF)


def exchange(value, axis):
    return lax.all_to_all(value, axis, 0, 0, tiled=True)


def tied(*values):
    return lax.optimization_barrier(values)


def pick_weight(core, got_ref, other_ref, mode, side):
    width = 32
    span = slice(side * width, (side + 1) * width)
    blocks = []
    for part in range(2):
        mine = got_ref[2 * mode + part, span, :]
        other = other_ref[2 * mode + part, span, :]
        blocks.append(jnp.where(core == 0, mine, other))
        blocks.append(jnp.where(core == 0, other, mine))
    return jnp.concatenate(blocks, 0)


def middle_kernel(
    core_ref,
    got_ref,
    other_ref,
    low_ref,
    wide_ref,
    high_ref,
    cot_ref,
    conv_ref,
    table_ref,
    grad_ref,
    sent_ref,
    spec_ref,
    mix_ref,
    turn_ref,
    sum_ref,
):
    modes = table_ref.shape[0] // 4
    forward_tab = table_ref[: 2 * modes, :]
    back = table_ref[2 * modes :, :]
    inverse_tab = back.astype(F32).T.astype(BF)
    near = grad_ref.shape[0]
    cells = near - 2
    bins, chans = grad_ref.shape[1:]
    rows = spec_ref.shape[1]
    band = 32
    core = core_ref[0]
    sum_ref[...] = jnp.zeros_like(sum_ref)
    spec_ref[:, near:, :] = jnp.zeros((2 * modes, rows - near, chans), F32)
    for cell in range(near):
        spec_ref[:, cell, :] = jnp.dot(
            forward_tab, wide_ref[cell + 1], preferred_element_type=F32
        )

    def mix_one(mode, carry):
        lhs = jnp.concatenate([spec_ref[mode], spec_ref[modes + mode]], 0).astype(BF)
        by_real, by_imag = [
            jnp.dot(
                lhs,
                pick_weight(core, got_ref, other_ref, mode, side),
                preferred_element_type=F32,
            )
            for side in range(2)
        ]
        mix_ref[:, mode, :] = by_real[:rows] - by_imag[rows:]
        mix_ref[:, modes + mode, :] = by_imag[:rows] + by_real[rows:]
        return carry

    lax.fori_loop(0, modes, mix_one, 0, unroll=4)

    def one_cell(cell, own):
        spectral = jnp.dot(inverse_tab, mix_ref[cell].astype(BF), preferred_element_type=F32)
        pieces = []
        for start in range(0, bins, band):
            span = slice(start, start + band)
            total = spectral[span]
            windows = []
            for row, ref in enumerate((low_ref, wide_ref, high_ref)):
                for col in range(3):
                    window = ref[cell + col, span, :].astype(F32)
                    windows.append(window)
                    total = total + window * conv_ref[3 * row + col : 3 * row + col + 1, :]
            activ, slope = gelu_pair(total)
            cot = cot_ref[cell, span, :]
            grad = (cot * conv_ref[9:10, :] * slope).astype(BF)
            pieces.append(grad)
            if own:
                wide_grad = grad.astype(F32)
                for index_d, window in enumerate(windows + [None]):
                    term = cot * activ if window is None else window * wide_grad
                    sum_ref[index_d] += jnp.sum(term.reshape(band // 8, 8, chans), 0)
        grad = jnp.concatenate(pieces, 0)
        grad_ref[cell] = grad
        return grad

    one_cell(0, False)
    one_cell(near - 1, False)

    def own_cell(cell, carry):
        grad = one_cell(cell + 1, True)
        turn_ref[:, cell, :] = jnp.dot(back, grad, preferred_element_type=F32)
        return carry

    lax.fori_loop(0, cells, own_cell, 0)
    small = [jnp.sum(sum_ref[index_d], 0, keepdims=True) for index_d in range(10)]
    small = jnp.concatenate(small + [jnp.zeros((6, chans), F32)], 0).astype(BF)

    def pack_one(mode, carry):
        pair = jnp.concatenate([turn_ref[mode], turn_ref[modes + mode]], 0).astype(BF)
        for part in range(2):
            sent_ref[2 * mode + part, 0:16, :] = pair
            sent_ref[2 * mode + part, 16:32, :] = small
        return carry

    lax.fori_loop(0, modes, pack_one, 0, unroll=4)


def last_kernel(
    core_ref,
    got_ref,
    other_ref,
    sent_ref,
    low_ref,
    wide_ref,
    high_ref,
    conv_ref,
    table_ref,
    out_ref,
    stack_ref,
):
    modes = table_ref.shape[0] // 4
    forward_turn = table_ref[: 2 * modes, :].astype(F32).T.astype(BF)
    cells, bins, chans = out_ref.shape
    band = 32
    core = core_ref[0]

    def mix_one(mode, carry):
        lhs = sent_ref[2 * mode, 0:16, :]
        by_real, by_imag = [
            lax.dot_general(
                lhs,
                pick_weight(core, got_ref, other_ref, mode, side),
                (((1,), (1,)), ((), ())),
                preferred_element_type=F32,
            )
            for side in range(2)
        ]
        stack_ref[:, mode, :] = by_real[:cells] + by_imag[cells:]
        stack_ref[:, modes + mode, :] = by_real[cells:] - by_imag[:cells]
        return carry

    lax.fori_loop(0, modes, mix_one, 0, unroll=4)

    def one_cell(cell, carry):
        total = jnp.dot(forward_turn, stack_ref[cell].astype(BF), preferred_element_type=F32)
        for start in range(0, bins, band):
            span = slice(start, start + band)
            part = total[span]
            for row, ref in enumerate((high_ref, wide_ref, low_ref)):
                for col in range(3):
                    window = ref[cell + 2 - col, span, :].astype(F32)
                    part = part + window * conv_ref[3 * row + col : 3 * row + col + 1, :]
            out_ref[cell, span, :] = part
        return carry

    lax.fori_loop(0, cells, one_cell, 0)


def on_core(kernel, operands, out_shape, scratch):
    whole = pl.BlockSpec(memory_space=pltpu.VMEM)
    return pl.pallas_call(
        kernel,
        out_shape=out_shape,
        in_specs=[pl.BlockSpec(memory_space=pltpu.SMEM)] + [whole] * (len(operands) - 1),
        out_specs=jax.tree.map(lambda _: whole, out_shape),
        scratch_shapes=scratch,
        compiler_params=pltpu.CompilerParams(vmem_limit_bytes=20 * 1024 * 1024),
        cost_estimate=pl.CostEstimate(
            flops=200_000_000, bytes_accessed=12_000_000, transcendentals=400_000
        ),
    )(*operands)


def local(hidden, cotangent, spectral_w, conv_k, proj_w):
    rows_here, cols, bins, chans = hidden.shape
    groups = lax.axis_size("grp")
    tiles = lax.axis_size("tile")
    half = spectral_w.shape[0]
    modes = half * tiles // chans
    parts = chans // half
    cells = rows_here * cols
    core = lax.axis_index("grp") % 2
    which = core.astype(jnp.int32).reshape(1)
    quarter = half // 2
    near = cols + 2
    count = conv_k.shape[0] + 1
    tables = spectral_tables(modes, bins)
    gains = jnp.concatenate([conv_k, proj_w[None], jnp.zeros((6, chans), F32)], 0)
    own_rows = lax.dynamic_slice_in_dim(spectral_w, core * quarter, quarter, 0)
    own_rows = jnp.concatenate([own_rows[:, :chans], own_rows[:, chans:]], 0)
    sent = (
        to_spec(tables[: 2 * modes], hidden[0])
        .reshape(2, modes, cells, parts, half)
        .transpose(1, 3, 2, 0, 4)
        .reshape(tiles, cells, 2 * half)
    )
    sent = jnp.concatenate([jnp.broadcast_to(own_rows, (tiles,) + own_rows.shape), sent], 1)
    sent, hidden, cotangent = tied(sent, hidden, cotangent)
    got = exchange(sent, "tile")
    low_t = shifted(edge_pack(hidden[0, cols - 2 :], split3(cotangent[0, cols - 1])), "tile", 1)
    high_t = shifted(edge_pack(hidden[0, :2], split3(cotangent[0, 0])), "tile", -1)
    got, low_t, high_t = tied(got, low_t, high_t)
    low_cols, low_cot = edge_unpack(low_t, bins)
    high_cols, high_cot = edge_unpack(high_t, bins)
    wide = jnp.concatenate([low_cols, hidden[0], high_cols], 0)
    cot_wide = jnp.concatenate([low_cot, cotangent[0], high_cot], 0)
    cot_lanes = jnp.broadcast_to(cot_wide[:, :, None], (near, bins, chans))
    low_g = shifted(wide, "grp", 1)
    high_g = shifted(wide, "grp", -1)
    swap = [(i, i ^ 1) for i in range(groups)]
    other = lax.ppermute(got, "grp", swap)
    grad_wide, grad_sent = on_core(
        middle_kernel,
        (
            which,
            got,
            other,
            low_g,
            wide,
            high_g,
            cot_lanes,
            gains,
            tables,
        ),
        (
            jax.ShapeDtypeStruct((near, bins, chans), BF),
            jax.ShapeDtypeStruct((tiles, 32, chans), BF),
        ),
        [
            pltpu.VMEM((2 * modes, 16, chans), F32),
            pltpu.VMEM((16, 2 * modes, chans), F32),
            pltpu.VMEM((2 * modes, cells, chans), F32),
            pltpu.VMEM((count, 8, chans), F32),
        ],
    )
    low_gg = shifted(grad_wide, "grp", 1)
    high_gg = shifted(grad_wide, "grp", -1)
    got_g = exchange(grad_sent, "tile")
    own_h, _ = tied(got[:, 2 * quarter :], grad_sent)
    got_g, low_gg, high_gg = tied(got_g, low_gg, high_gg)
    lane = lax.broadcasted_iota(jnp.int32, own_h.shape, 2)
    left = jnp.concatenate([jnp.where(lane < half, own_h, -own_h), jnp.roll(own_h, half, 2)], 1)
    weight_part = lax.dot_general(
        left.reshape(tiles * 2 * cells, 2 * half),
        got_g[:, : 2 * cells].reshape(tiles * 2 * cells, chans),
        (((0,), (0,)), ((), ())),
        preferred_element_type=F32,
    ).astype(BF)
    totals = jnp.sum(got_g[:, 2 * cells : 2 * cells + count].astype(F32), 0)
    totals = split3(totals).reshape(3 * count, chans)
    grad_hidden = on_core(
        last_kernel,
        (
            which,
            got,
            other,
            grad_sent,
            low_gg,
            grad_wide,
            high_gg,
            gains,
            tables,
        ),
        jax.ShapeDtypeStruct((cells, bins, chans), F32),
        [pltpu.VMEM((cells, 2 * modes, chans), F32)],
    ).reshape(rows_here, cols, bins, chans)
    last = jnp.concatenate([weight_part, totals], 0)
    last = exchange(jnp.broadcast_to(last, (groups,) + last.shape), "grp")
    grad_spectral = jnp.sum(last[:, : 2 * half].astype(F32), 0)
    grad_spectral = jnp.concatenate([grad_spectral[:half], grad_spectral[half:]], 1)
    totals = last[:, 2 * half :].astype(F32).reshape(groups, 3, count, chans)
    totals = jnp.sum(totals, (0, 1))
    return (grad_hidden, grad_spectral, totals[: count - 1], totals[count - 1])


def solution(mesh):
    in_specs = (P("grp", "tile", None, None), P("grp", "tile", None), P("tile", None), P(), P())
    out_specs = (P("grp", "tile", None, None), P("tile", None), P(), P())
    return jax.shard_map(local, mesh=mesh, in_specs=in_specs, out_specs=out_specs, check_vma=False)
```

time: 146 us -> 128 us (0.88)
  starting transfers between devices: 87.9 us -> 59.1 us
  Pallas kernels: 0 us -> 11.4 us
  waiting for transfers between devices: 41.7 us -> 44.9 us
  matrix products: 5.2 us -> 2.57 us
  local copies, waits for them, and re-layouts: 6.51 us -> 4.21 us
    all_to_all x5 -> x3, starting transfers between devices: 59.1 us -> 33.5 us  [exchange(): return lax.all_to_all(value, axis, 0, 0, tiled=True)]
    ppermute x8 -> x7, waiting for transfers between devices: 11.3 us -> 35.4 us  [the longest x6 35.4 us: shifted(): return lax.ppermute(block, axis, pairs)]
    all_to_all x5 -> x3, waiting for transfers between devices: 30.4 us -> 9.43 us  [exchange(): return lax.all_to_all(value, axis, 0, 0, tiled=True)]
    pallas_call x0 -> x2, Pallas kernels: none -> 11.4 us  [on_core(): pl.pallas_call(kernel, out_shape=out_shape, in_specs=[pl.BlockSpec(memory...]
    ppermute x8 -> x7, starting transfers between devices: 28.8 us -> 25.6 us  [the longest x6 17.4 us: shifted(): return lax.ppermute(block, axis, pairs)]
    dot_general x7 -> x2, matrix products: 5.2 us -> 2.57 us  [the longest x1 1.43 us: local(): lax.dot_general(left.reshape(tiles * 2 * cells, 2 * half), got_g[:, :2 *...]
  transfers between devices with their start and end apart: 13 -> 10, of which waited for: 11 -> 8; matrix products, arithmetic and copies ran while one was open for 3% -> 1% of each run, Pallas kernels for 0% -> 4%
where the time goes in v2:
time: 128 us; the launch traced here: 127 us
  starting transfers between devices  59.1 us (46%)
  waiting for transfers between devices  44.9 us (35%)
  Pallas kernels  11.4 us (9%)
  local copies, waits for them, and re-layouts  4.21 us (3%)
  other arithmetic  4.05 us (3%)
  matrix products  2.57 us (2%)
    ppermute x6, waiting for transfers between devices, shifted(): return lax.ppermute(block, axis, pairs)  35.4 us
    all_to_all x3, starting transfers between devices, exchange(): return lax.all_to_all(value, axis, 0, 0, tiled=True)  33.5 us
    ppermute x6, starting transfers between devices, shifted(): return lax.ppermute(block, axis, pairs)  17.4 us
    pallas_call x2, Pallas kernels, on_core(): pl.pallas_call(kernel, out_shape=out_shape, in_specs=[pl.BlockSpec(memory...  11.4 us
    all_to_all x3, waiting for transfers between devices, exchange(): return lax.all_to_all(value, axis, 0, 0, tiled=True)  9.43 us
    ppermute x1, starting transfers between devices, local(): other = lax.ppermute(got, 'grp', swap)  8.27 us
  transfers between devices with their start and end apart: 10, of which 8 were waited for; matrix products, arithmetic and copies ran while one was open for 1% of the time, Pallas kernels for 4%

profile of v2, /device:TPU:1, one launch (start us, length us, event | category | flops | bytes accessed | tf_op | source)
XLA Modules:
  0.0 127.2 jit_solution(16941462961503898989)
XLA Ops:
  0.7 1.1 convolution_convert_fusion
  2.7 1.1 pad_maximum_fusion
  3.8 19.7 %all-to-all-start = ((bf16[64,72,128]{2,1,0:T(8,128)(2,1)}), bf16[64,72,128]{2,1,0:T(8,128)(2,1)S(1)}, u32[]{:S(2)}, u32[]{:S(2)}) async-start(bf16[64,72,128]{2,1,0:T(8,128)(2,1)} %pad_maximum_fusion), calls=%async_computation | async-start | bytes 2359296 | tf_op jit(solution)/shard_map/all_to_all | solution.py:63
  23.7 1.3 %collective-permute-start.1 = (bf16[264,128]{1,0:T(8,128)(2,1)S(1)}, bf16[264,128]{1,0:T(8,128)(2,1)S(1)}, u32[]{:S(2)}, u32[]{:S(2)}) collective-permute-start(bf16[264,128]{1,0:T(8,128)(2,1)S(1)} %concatenate.39), channel_id=1, source_target_pairs={{1,0},{2,1},{3,2},{4,3},{5,4},{6,5},{7,6},{8,7},{9,8},{10,9},{11,1... | collective-permute-start | bytes 202760 | tf_op jit(solution)/shard_map/ppermute | solution.py:16
  25.0 4.0 %collective-permute-start = (bf16[264,128]{1,0:T(8,128)(2,1)S(1)}, bf16[264,128]{1,0:T(8,128)(2,1)S(1)}, u32[]{:S(2)}, u32[]{:S(2)}) collective-permute-start(bf16[264,128]{1,0:T(8,128)(2,1)S(1)} %concatenate.38), channel_id=1, source_target_pairs={{0,1},{1,2},{2,3},{3,4},{4,5},{5,6},{6,7},{7,8},{8,9},{9,10},{10,1... | collective-permute-start | bytes 202760 | tf_op jit(solution)/shard_map/ppermute | solution.py:16
  29.0 21.2 %collective-permute-done.1 = bf16[264,128]{1,0:T(8,128)(2,1)S(1)} collective-permute-done((bf16[264,128]{1,0:T(8,128)(2,1)S(1)}, bf16[264,128]{1,0:T(8,128)(2,1)S(1)}, u32[]{:S(2)}, u32[]{:S(2)}) %collective-permute-start.1) | collective-permute-done | bytes 67616 | tf_op jit(solution)/shard_map/ppermute | solution.py:16
  50.2 1.6 %all-to-all-done.got_ref = bf16[64,72,128]{2,1,0:T(8,128)(2,1)S(1)} async-done(((bf16[64,72,128]{2,1,0:T(8,128)(2,1)}), bf16[64,72,128]{2,1,0:T(8,128)(2,1)S(1)}, u32[]{:S(2)}, u32[]{:S(2)}) %all-to-all-start) | async-done | bytes 1179680 | tf_op jit(solution)/shard_map/all_to_all | solution.py:63
  51.7 8.3 %collective-permute-start.2 = (bf16[64,72,128]{2,1,0:T(8,128)(2,1)S(1)}, bf16[64,72,128]{2,1,0:T(8,128)(2,1)S(1)}, u32[]{:S(2)}, u32[]{:S(2)}) collective-permute-start(bf16[64,72,128]{2,1,0:T(8,128)(2,1)S(1)} %all-to-all-done.got_ref), channel_id=1, source_target_pairs={{0,64},{64,0},{128,192},{192,128},{256,320},{320,256},{384,448},{4... | collective-permute-start | bytes 3538952 | tf_op jit(solution)/shard_map/ppermute | solution.py:282
  60.2 5.8 %collective-permute-start.3 = (bf16[12,128,128]{2,1,0:T(8,128)(2,1)S(1)}, bf16[12,128,128]{2,1,0:T(8,128)(2,1)S(1)}, u32[]{:S(2)}, u32[]{:S(2)}) collective-permute-start(bf16[12,128,128]{2,1,0:T(8,128)(2,1)S(1)} %pad_maximum_fusion.1.wide_ref), channel_id=1, source_target_pairs={{0,64},{64,128},{128,192},{192,256},{256,320},{320,384},{384,448},... | collective-permute-start | bytes 1179656 | tf_op jit(solution)/shard_map/ppermute | solution.py:16
  66.0 1.9 %collective-permute-start.4 = (bf16[12,128,128]{2,1,0:T(8,128)(2,1)S(1)}, bf16[12,128,128]{2,1,0:T(8,128)(2,1)S(1)}, u32[]{:S(2)}, u32[]{:S(2)}) collective-permute-start(bf16[12,128,128]{2,1,0:T(8,128)(2,1)S(1)} %pad_maximum_fusion.1.wide_ref), channel_id=1, source_target_pairs={{64,0},{128,64},{192,128},{256,192},{320,256},{384,320},{448,384},... | collective-permute-start | bytes 1179656 | tf_op jit(solution)/shard_map/ppermute | solution.py:16
  68.1 2.6 %collective-permute-done.3.low_ref = bf16[12,128,128]{2,1,0:T(8,128)(2,1)S(1)} collective-permute-done((bf16[12,128,128]{2,1,0:T(8,128)(2,1)S(1)}, bf16[12,128,128]{2,1,0:T(8,128)(2,1)S(1)}, u32[]{:S(2)}, u32[]{:S(2)}) %collective-permute-start.3) | collective-permute-done | bytes 393248 | tf_op jit(solution)/shard_map/ppermute | solution.py:16
  70.7 4.4 %collective-permute-done.4.high_ref = bf16[12,128,128]{2,1,0:T(8,128)(2,1)S(1)} collective-permute-done((bf16[12,128,128]{2,1,0:T(8,128)(2,1)S(1)}, bf16[12,128,128]{2,1,0:T(8,128)(2,1)S(1)}, u32[]{:S(2)}, u32[]{:S(2)}) %collective-permute-start.4) | collective-permute-done | bytes 393248 | tf_op jit(solution)/shard_map/ppermute | solution.py:16
  75.4 6.1 %shard_map.93 = (bf16[10,128,128]{2,1,0:T(8,128)(2,1)S(1)}, bf16[64,32,128]{2,1,0:T(8,128)(2,1)}) custom-call(s32[1]{0:T(128)} %bitcast.core_ref, bf16[64,72,128]{2,1,0:T(8,128)(2,1)S(1)} %all-to-all-done.got_ref, bf16[64,72,128]{2,1,0:T(8,128)(2,1)S(1)} %collective-permute-done.2.other_ref, bf16[12,128,128]{2,1,0:T(8,128)(2,1)S(1)} %collective-permute-done.3.low_ref, ...), custom_call_target="tpu_custom_call" | custom-call | flops 200000000 | bytes 12000000 | tf_op jit(solution)/shard_map/pallas_call | solution.py:232
  81.5 6.1 %all-to-all-start.1 = ((bf16[64,32,128]{2,1,0:T(8,128)(2,1)}), bf16[64,32,128]{2,1,0:T(8,128)(2,1)}, u32[]{:S(2)}, u32[]{:S(2)}) async-start(bf16[64,32,128]{2,1,0:T(8,128)(2,1)} %get-tuple-element.22.sent_ref), calls=%async_computation.1 | async-start | bytes 1048576 | tf_op jit(solution)/shard_map/all_to_all | solution.py:63
  87.6 2.0 %collective-permute-start.5 = (bf16[10,128,128]{2,1,0:T(8,128)(2,1)S(1)}, bf16[10,128,128]{2,1,0:T(8,128)(2,1)S(1)}, u32[]{:S(2)}, u32[]{:S(2)}) collective-permute-start(bf16[10,128,128]{2,1,0:T(8,128)(2,1)S(1)} %get-tuple-element.23.wide_ref), channel_id=1, source_target_pairs={{0,64},{64,128},{128,192},{192,256},{256,320},{320,384},{384,448},... | collective-permute-start | bytes 983048 | tf_op jit(solution)/shard_map/ppermute | solution.py:16
  89.7 2.3 %collective-permute-start.6 = (bf16[10,128,128]{2,1,0:T(8,128)(2,1)S(1)}, bf16[10,128,128]{2,1,0:T(8,128)(2,1)S(1)}, u32[]{:S(2)}, u32[]{:S(2)}) collective-permute-start(bf16[10,128,128]{2,1,0:T(8,128)(2,1)S(1)} %get-tuple-element.23.wide_ref), channel_id=1, source_target_pairs={{64,0},{128,64},{192,128},{256,192},{320,256},{384,320},{448,384},... | collective-permute-start | bytes 983048 | tf_op jit(solution)/shard_map/ppermute | solution.py:16
  92.8 6.7 %collective-permute-done.5.low_ref = bf16[10,128,128]{2,1,0:T(8,128)(2,1)S(1)} collective-permute-done((bf16[10,128,128]{2,1,0:T(8,128)(2,1)S(1)}, bf16[10,128,128]{2,1,0:T(8,128)(2,1)S(1)}, u32[]{:S(2)}, u32[]{:S(2)}) %collective-permute-start.5) | collective-permute-done | bytes 327712 | tf_op jit(solution)/shard_map/ppermute | solution.py:16
  100.0 3.0 %all-to-all-done.1 = bf16[64,32,128]{2,1,0:T(8,128)(2,1)} async-done(((bf16[64,32,128]{2,1,0:T(8,128)(2,1)}), bf16[64,32,128]{2,1,0:T(8,128)(2,1)}, u32[]{:S(2)}, u32[]{:S(2)}) %all-to-all-start.1) | async-done | bytes 524320 | tf_op jit(solution)/shard_map/all_to_all | solution.py:63
  103.0 1.0 convert_reduce_fusion.1
  104.1 1.4 %fusion = bf16[128,128]{1,0:T(8,128)(2,1)S(1)} fusion(bf16[64,8,64]{2,1,0:T(8,128)(2,1)} %get-tuple-element.31, bf16[64,8,64]{2,1,0:T(8,128)(2,1)} %get-tuple-element.30, bf16[64,8,128]{2,1,0:T(8,128)(2,1)S(1)} %negate_select_fusion, bf16[64,32,128]{2,1,0:T(8,128)(2,1)} %all-to-all-done.1), kind=kOutput, calls=%fused_computation.3 | convolution fusion | flops 34357248 | bytes 688128 | tf_op jit(solution)/shard_map/dot_general | solution.py:314
  106.3 7.7 %all-to-all-start.2 = ((bf16[8,158,128]{2,1,0:T(8,128)(2,1)}), bf16[8,158,128]{2,1,0:T(8,128)(2,1)}, u32[]{:S(2)}, u32[]{:S(2)}) async-start(bf16[8,158,128]{2,1,0:T(8,128)(2,1)} %broadcast_in_dim.30), calls=%async_computation.2 | async-start | bytes 655360 | tf_op jit(solution)/shard_map/all_to_all | solution.py:63
  114.0 5.2 %shard_map.94 = f32[8,128,128]{2,1,0:T(8,128)} custom-call(s32[1]{0:T(128)} %bitcast.core_ref, bf16[64,72,128]{2,1,0:T(8,128)(2,1)S(1)} %all-to-all-done.got_ref, bf16[64,72,128]{2,1,0:T(8,128)(2,1)S(1)} %collective-permute-done.2.other_ref, bf16[64,32,128]{2,1,0:T(8,128)(2,1)} %get-tuple-element.22.sent_ref, ...), custom_call_target="tpu_custom_call" | custom-call | flops 200000000 | bytes 12000000 | tf_op jit(solution)/shard_map/pallas_call | solution.py:232
  119.2 4.9 %all-to-all-done.2 = bf16[8,158,128]{2,1,0:T(8,128)(2,1)} async-done(((bf16[8,158,128]{2,1,0:T(8,128)(2,1)}), bf16[8,158,128]{2,1,0:T(8,128)(2,1)}, u32[]{:S(2)}, u32[]{:S(2)}) %all-to-all-start.2) | async-done | bytes 323616 | tf_op jit(solution)/shard_map/all_to_all | solution.py:63
  124.1 1.0 convert_reduce_fusion
  (53 shorter events, 5.6 us)
Async XLA Ops:
  0.6 1.8 %copy-start.2 = (bf16[64,256]{1,0:T(8,128)(2,1)S(1)}, bf16[64,256]{1,0:T(8,128)(2,1)}, u32[]{:S(2)}) copy-start(bf16[64,256]{1,0:T(8,128)(2,1)} %param.8) | copy-start | bytes 98308
  3.8 19.7 %copy-start.5 = (f32[1,8,128]{2,1,0:T(8,128)S(1)}, f32[1,8,128]{2,1,0:T(8,128)}, u32[]{:S(2)}) copy-start(f32[1,8,128]{2,1,0:T(8,128)} %param.7) | copy-start | bytes 12292
  3.8 19.8 %copy-start.1 = (bf16[1,8,128,128]{3,2,1,0:T(8,128)(2,1)S(1)}, bf16[1,8,128,128]{3,2,1,0:T(8,128)(2,1)}, u32[]{:S(2)}) copy-start(bf16[1,8,128,128]{3,2,1,0:T(8,128)(2,1)} %param.6) | copy-start | bytes 786436
  3.8 47.9 %all-to-all-start = ((bf16[64,72,128]{2,1,0:T(8,128)(2,1)}), bf16[64,72,128]{2,1,0:T(8,128)(2,1)S(1)}, u32[]{:S(2)}, u32[]{:S(2)}) async-start(bf16[64,72,128]{2,1,0:T(8,128)(2,1)} %pad_maximum_fusion), calls=%async_computation | async-start | bytes 2359296 | tf_op jit(solution)/shard_map/all_to_all | solution.py:63
  23.5 44.4 %copy-start.3 = (f32[9,128]{1,0:T(8,128)S(1)}, f32[9,128]{1,0:T(8,128)}, u32[]{:S(2)}) copy-start(f32[9,128]{1,0:T(8,128)} %param.9) | copy-start | bytes 13828
  23.6 44.4 %copy-start.6 = (f32[128]{0:T(128)S(1)}, f32[128]{0:T(128)}, u32[]{:S(2)}) copy-start(f32[128]{0:T(128)} %param.10) | copy-start | bytes 1540
  23.6 51.8 %copy-start = (bf16[128,128]{1,0:T(8,128)(2,1)S(1)}, bf16[128,128]{1,0:T(8,128)(2,1)}, u32[]{:S(2)}) copy-start(bf16[128,128]{1,0:T(8,128)(2,1)} %constant.32.clone.table_ref) | copy-start | bytes 98308
  23.7 26.5 %collective-permute-start.1 = (bf16[264,128]{1,0:T(8,128)(2,1)S(1)}, bf16[264,128]{1,0:T(8,128)(2,1)S(1)}, u32[]{:S(2)}, u32[]{:S(2)}) collective-permute-start(bf16[264,128]{1,0:T(8,128)(2,1)S(1)} %concatenate.39), channel_id=1, source_target_pairs={{1,0},{2,1},{3,2},{4,3},{5,4},{6,5},{7,6},{8,7},{9,8},{10,9},{11,1... | collective-permute-start | bytes 202760 | tf_op jit(solution)/shard_map/ppermute | solution.py:16
  25.0 25.2 %collective-permute-start = (bf16[264,128]{1,0:T(8,128)(2,1)S(1)}, bf16[264,128]{1,0:T(8,128)(2,1)S(1)}, u32[]{:S(2)}, u32[]{:S(2)}) collective-permute-start(bf16[264,128]{1,0:T(8,128)(2,1)S(1)} %concatenate.38), channel_id=1, source_target_pairs={{0,1},{1,2},{2,3},{3,4},{4,5},{5,6},{6,7},{7,8},{8,9},{9,10},{10,1... | collective-permute-start | bytes 202760 | tf_op jit(solution)/shard_map/ppermute | solution.py:16
  51.7 23.4 %collective-permute-start.2 = (bf16[64,72,128]{2,1,0:T(8,128)(2,1)S(1)}, bf16[64,72,128]{2,1,0:T(8,128)(2,1)S(1)}, u32[]{:S(2)}, u32[]{:S(2)}) collective-permute-start(bf16[64,72,128]{2,1,0:T(8,128)(2,1)S(1)} %all-to-all-done.got_ref), channel_id=1, source_target_pairs={{0,64},{64,0},{128,192},{192,128},{256,320},{320,256},{384,448},{4... | collective-permute-start | bytes 3538952 | tf_op jit(solution)/shard_map/ppermute | solution.py:282
  60.2 10.6 %collective-permute-start.3 = (bf16[12,128,128]{2,1,0:T(8,128)(2,1)S(1)}, bf16[12,128,128]{2,1,0:T(8,128)(2,1)S(1)}, u32[]{:S(2)}, u32[]{:S(2)}) collective-permute-start(bf16[12,128,128]{2,1,0:T(8,128)(2,1)S(1)} %pad_maximum_fusion.1.wide_ref), channel_id=1, source_target_pairs={{0,64},{64,128},{128,192},{192,256},{256,320},{320,384},{384,448},... | collective-permute-start | bytes 1179656 | tf_op jit(solution)/shard_map/ppermute | solution.py:16
  66.0 9.1 %collective-permute-start.4 = (bf16[12,128,128]{2,1,0:T(8,128)(2,1)S(1)}, bf16[12,128,128]{2,1,0:T(8,128)(2,1)S(1)}, u32[]{:S(2)}, u32[]{:S(2)}) collective-permute-start(bf16[12,128,128]{2,1,0:T(8,128)(2,1)S(1)} %pad_maximum_fusion.1.wide_ref), channel_id=1, source_target_pairs={{64,0},{128,64},{192,128},{256,192},{320,256},{384,320},{448,384},... | collective-permute-start | bytes 1179656 | tf_op jit(solution)/shard_map/ppermute | solution.py:16
  81.5 21.5 %all-to-all-start.1 = ((bf16[64,32,128]{2,1,0:T(8,128)(2,1)}), bf16[64,32,128]{2,1,0:T(8,128)(2,1)}, u32[]{:S(2)}, u32[]{:S(2)}) async-start(bf16[64,32,128]{2,1,0:T(8,128)(2,1)} %get-tuple-element.22.sent_ref), calls=%async_computation.1 | async-start | bytes 1048576 | tf_op jit(solution)/shard_map/all_to_all | solution.py:63
  87.6 11.9 %collective-permute-start.5 = (bf16[10,128,128]{2,1,0:T(8,128)(2,1)S(1)}, bf16[10,128,128]{2,1,0:T(8,128)(2,1)S(1)}, u32[]{:S(2)}, u32[]{:S(2)}) collective-permute-start(bf16[10,128,128]{2,1,0:T(8,128)(2,1)S(1)} %get-tuple-element.23.wide_ref), channel_id=1, source_target_pairs={{0,64},{64,128},{128,192},{192,256},{256,320},{320,384},{384,448},... | collective-permute-start | bytes 983048 | tf_op jit(solution)/shard_map/ppermute | solution.py:16
  89.7 10.3 %collective-permute-start.6 = (bf16[10,128,128]{2,1,0:T(8,128)(2,1)S(1)}, bf16[10,128,128]{2,1,0:T(8,128)(2,1)S(1)}, u32[]{:S(2)}, u32[]{:S(2)}) collective-permute-start(bf16[10,128,128]{2,1,0:T(8,128)(2,1)S(1)} %get-tuple-element.23.wide_ref), channel_id=1, source_target_pairs={{64,0},{128,64},{192,128},{256,192},{320,256},{384,320},{448,384},... | collective-permute-start | bytes 983048 | tf_op jit(solution)/shard_map/ppermute | solution.py:16
  106.3 17.8 %all-to-all-start.2 = ((bf16[8,158,128]{2,1,0:T(8,128)(2,1)}), bf16[8,158,128]{2,1,0:T(8,128)(2,1)}, u32[]{:S(2)}, u32[]{:S(2)}) async-start(bf16[8,158,128]{2,1,0:T(8,128)(2,1)} %broadcast_in_dim.30), calls=%async_computation.2 | async-start | bytes 655360 | tf_op jit(solution)/shard_map/all_to_all | solution.py:63
  126.0 1.2 copy-start.4

commit v3 on v2

--- a/solution.py
+++ b/solution.py
@@ -14,6 +14,24 @@
     count = lax.axis_size(axis)
     pairs = [(i, i + step) for i in range(count) if 0 <= i + step < count]
     return lax.ppermute(block, axis, pairs)
+
+
+def mate(block):
+    return lax.ppermute(block, "grp", [(i, i ^ 1) for i in range(lax.axis_size("grp"))])
+
+
+def across(block, step):
+    rows, cols = lax.axis_size("grp"), lax.axis_size("tile")
+    pairs = []
+    for row in range(rows):
+        far = row + 1 if row % 2 else row - 1
+        if 0 <= far < rows:
+            pairs += [
+                (row * cols + col, far * cols + col + step)
+                for col in range(cols)
+                if 0 <= col + step < cols
+            ]
+    return lax.ppermute(block, ("grp", "tile"), pairs)
 
 
 def edge_pack(columns, cot):
@@ -83,9 +101,9 @@
     core_ref,
     got_ref,
     other_ref,
-    low_ref,
+    far_ref,
     wide_ref,
-    high_ref,
+    close_ref,
     cot_ref,
     conv_ref,
     table_ref,
@@ -136,7 +154,7 @@
             span = slice(start, start + band)
             total = spectral[span]
             windows = []
-            for row, ref in enumerate((low_ref, wide_ref, high_ref)):
+            for row, ref in enumerate((far_ref, wide_ref, close_ref)):
                 for col in range(3):
                     window = ref[cell + col, span, :].astype(F32)
                     windows.append(window)
@@ -164,7 +182,17 @@
 
     lax.fori_loop(0, cells, own_cell, 0)
     small = [jnp.sum(sum_ref[index_d], 0, keepdims=True) for index_d in range(10)]
-    small = jnp.concatenate(small + [jnp.zeros((6, chans), F32)], 0).astype(BF)
+    upper, lower = jnp.concatenate(small[:3], 0), jnp.concatenate(small[6:9], 0)
+    small = jnp.concatenate(
+        [
+            jnp.where(core == 0, upper, lower),
+            *small[3:6],
+            jnp.where(core == 0, lower, upper),
+            small[9],
+            jnp.zeros((6, chans), F32),
+        ],
+        0,
+    ).astype(BF)
 
     def pack_one(mode, carry):
         pair = jnp.concatenate([turn_ref[mode], turn_ref[modes + mode]], 0).astype(BF)
@@ -181,9 +209,9 @@
     got_ref,
     other_ref,
     sent_ref,
-    low_ref,
+    far_ref,
     wide_ref,
-    high_ref,
+    close_ref,
     conv_ref,
     table_ref,
     out_ref,
@@ -217,7 +245,7 @@
         for start in range(0, bins, band):
             span = slice(start, start + band)
             part = total[span]
-            for row, ref in enumerate((high_ref, wide_ref, low_ref)):
+            for row, ref in enumerate((close_ref, wide_ref, far_ref)):
                 for col in range(3):
                     window = ref[cell + 2 - col, span, :].astype(F32)
                     part = part + window * conv_ref[3 * row + col : 3 * row + col + 1, :]
@@ -227,12 +255,44 @@
     lax.fori_loop(0, cells, one_cell, 0)
 
 
-def on_core(kernel, operands, out_shape, scratch):
+def gather_kernel(left_ref, got_ref, out_ref):
+    tiles, rows, width = left_ref.shape
+    chans = got_ref.shape[2]
+    term = lax.dot_general(
+        left_ref[...].reshape(tiles * rows, width),
+        got_ref[:, :rows, :].reshape(tiles * rows, chans),
+        (((0,), (0,)), ((), ())),
+        preferred_element_type=F32,
+    ).astype(BF)
+    total = jnp.sum(got_ref[:, rows:, :].astype(F32), 0)
+    pieces = [term]
+    for _ in range(3):
+        piece = total.astype(BF)
+        total = total - piece.astype(F32)
+        pieces.append(piece)
+    block = jnp.concatenate(pieces, 0)
+    for group in range(out_ref.shape[0]):
+        out_ref[group] = block
+
+
+def finish_kernel(last_ref, spectral_ref, conv_ref, proj_ref):
+    half, width = spectral_ref.shape
+    total = jnp.sum(last_ref[...].astype(F32), 0)
+    spectral_ref[:, : width // 2] = total[:half]
+    spectral_ref[:, width // 2 :] = total[half : 2 * half]
+    rest = total[2 * half :]
+    rest = rest[:16] + rest[16:32] + rest[32:]
+    conv_ref[...] = rest[:9]
+    proj_ref[...] = rest[9:10]
+
+
+def on_core(kernel, operands, out_shape, scratch=(), scalars=1):
     whole = pl.BlockSpec(memory_space=pltpu.VMEM)
     return pl.pallas_call(
         kernel,
         out_shape=out_shape,
-        in_specs=[pl.BlockSpec(memory_space=pltpu.SMEM)] + [whole] * (len(operands) - 1),
+        in_specs=[pl.BlockSpec(memory_space=pltpu.SMEM)] * scalars
+        + [whole] * (len(operands) - scalars),
         out_specs=jax.tree.map(lambda _: whole, out_shape),
         scratch_shapes=scratch,
         compiler_params=pltpu.CompilerParams(vmem_limit_bytes=20 * 1024 * 1024),
@@ -256,7 +316,17 @@
     near = cols + 2
     count = conv_k.shape[0] + 1
     tables = spectral_tables(modes, bins)
-    gains = jnp.concatenate([conv_k, proj_w[None], jnp.zeros((6, chans), F32)], 0)
+    upper, centre, lower = conv_k[:3], conv_k[3:6], conv_k[6:]
+    gains = jnp.concatenate(
+        [
+            jnp.where(core == 0, upper, lower),
+            centre,
+            jnp.where(core == 0, lower, upper),
+            proj_w[None],
+            jnp.zeros((6, chans), F32),
+        ],
+        0,
+    )
     own_rows = lax.dynamic_slice_in_dim(spectral_w, core * quarter, quarter, 0)
     own_rows = jnp.concatenate([own_rows[:, :chans], own_rows[:, chans:]], 0)
     sent = (
@@ -268,27 +338,28 @@
     sent = jnp.concatenate([jnp.broadcast_to(own_rows, (tiles,) + own_rows.shape), sent], 1)
     sent, hidden, cotangent = tied(sent, hidden, cotangent)
     got = exchange(sent, "tile")
-    low_t = shifted(edge_pack(hidden[0, cols - 2 :], split3(cotangent[0, cols - 1])), "tile", 1)
-    high_t = shifted(edge_pack(hidden[0, :2], split3(cotangent[0, 0])), "tile", -1)
-    got, low_t, high_t = tied(got, low_t, high_t)
+    head, tail = hidden[0, :2], hidden[0, cols - 2 :]
+    low_t = shifted(edge_pack(tail, split3(cotangent[0, cols - 1])), "tile", 1)
+    high_t = shifted(edge_pack(head, split3(cotangent[0, 0])), "tile", -1)
+    far = [across(tail, 1), across(hidden[0], 0), across(head, -1)]
+    got, low_t, high_t, far = tied(got, low_t, high_t, far)
+    far = jnp.concatenate(far, 0)
     low_cols, low_cot = edge_unpack(low_t, bins)
     high_cols, high_cot = edge_unpack(high_t, bins)
     wide = jnp.concatenate([low_cols, hidden[0], high_cols], 0)
     cot_wide = jnp.concatenate([low_cot, cotangent[0], high_cot], 0)
     cot_lanes = jnp.broadcast_to(cot_wide[:, :, None], (near, bins, chans))
-    low_g = shifted(wide, "grp", 1)
-    high_g = shifted(wide, "grp", -1)
-    swap = [(i, i ^ 1) for i in range(groups)]
-    other = lax.ppermute(got, "grp", swap)
+    other = mate(got)
+    close = mate(wide)
     grad_wide, grad_sent = on_core(
         middle_kernel,
         (
             which,
             got,
             other,
-            low_g,
+            far,
             wide,
-            high_g,
+            close,
             cot_lanes,
             gains,
             tables,
@@ -304,21 +375,20 @@
             pltpu.VMEM((count, 8, chans), F32),
         ],
     )
-    low_gg = shifted(grad_wide, "grp", 1)
-    high_gg = shifted(grad_wide, "grp", -1)
+    far_grad = across(grad_wide, 0)
+    close_grad = mate(grad_wide)
     got_g = exchange(grad_sent, "tile")
-    own_h, _ = tied(got[:, 2 * quarter :], grad_sent)
-    got_g, low_gg, high_gg = tied(got_g, low_gg, high_gg)
+    late, _ = tied(got, grad_sent)
+    own_h = late[:, 2 * quarter :]
+    got_g, far_grad, close_grad = tied(got_g, far_grad, close_grad)
     lane = lax.broadcasted_iota(jnp.int32, own_h.shape, 2)
     left = jnp.concatenate([jnp.where(lane < half, own_h, -own_h), jnp.roll(own_h, half, 2)], 1)
-    weight_part = lax.dot_general(
-        left.reshape(tiles * 2 * cells, 2 * half),
-        got_g[:, : 2 * cells].reshape(tiles * 2 * cells, chans),
-        (((0,), (0,)), ((), ())),
-        preferred_element_type=F32,
-    ).astype(BF)
-    totals = jnp.sum(got_g[:, 2 * cells : 2 * cells + count].astype(F32), 0)
-    totals = split3(totals).reshape(3 * count, chans)
+    last = on_core(
+        gather_kernel,
+        (left, got_g),
+        jax.ShapeDtypeStruct((groups, 2 * half + 48, chans), BF),
+        scalars=0,
+    )
     grad_hidden = on_core(
         last_kernel,
         (
@@ -326,22 +396,26 @@
             got,
             other,
             grad_sent,
-            low_gg,
+            far_grad,
             grad_wide,
-            high_gg,
+            close_grad,
             gains,
             tables,
         ),
         jax.ShapeDtypeStruct((cells, bins, chans), F32),
         [pltpu.VMEM((cells, 2 * modes, chans), F32)],
     ).reshape(rows_here, cols, bins, chans)
-    last = jnp.concatenate([weight_part, totals], 0)
-    last = exchange(jnp.broadcast_to(last, (groups,) + last.shape), "grp")
-    grad_spectral = jnp.sum(last[:, : 2 * half].astype(F32), 0)
-    grad_spectral = jnp.concatenate([grad_spectral[:half], grad_spectral[half:]], 1)
-    totals = last[:, 2 * half :].astype(F32).reshape(groups, 3, count, chans)
-    totals = jnp.sum(totals, (0, 1))
-    return (grad_hidden, grad_spectral, totals[: count - 1], totals[count - 1])
+    grad_spectral, grad_conv, grad_proj = on_core(
+        finish_kernel,
+        (exchange(last, "grp"),),
+        (
+            jax.ShapeDtypeStruct((half, 2 * chans), F32),
+            jax.ShapeDtypeStruct((count - 1, chans), F32),
+            jax.ShapeDtypeStruct((1, chans), F32),
+        ),
+        scalars=0,
+    )
+    return (grad_hidden, grad_spectral, grad_conv, grad_proj[0])
 
 
 def solution(mesh):

time: 128 us -> 123 us (0.961)
  waiting for transfers between devices: 44.9 us -> 33.6 us
  starting transfers between devices: 59.1 us -> 64.8 us
  Pallas kernels: 11.4 us -> 13.1 us
  local copies, waits for them, and re-layouts: 4.21 us -> 5.68 us
  matrix products: 2.57 us -> 1.14 us
    ppermute x6 -> x2, waiting for transfers between devices: 35.4 us -> 0.01 us  [shifted(): return lax.ppermute(block, axis, pairs)]
    ppermute x1 -> x7, waiting for transfers between devices: 0.01 us -> 29.8 us  [the longest x4 29.8 us: across(): return lax.ppermute(block, ('grp', 'tile'), pairs)]
    ppermute x6 -> x2, starting transfers between devices: 17.4 us -> 5.88 us  [shifted(): return lax.ppermute(block, axis, pairs)]
    ppermute x1 -> x7, starting transfers between devices: 8.27 us -> 19.7 us  [the longest x4 10.9 us: across(): return lax.ppermute(block, ('grp', 'tile'), pairs)]
    all_to_all x3, starting transfers between devices: 33.5 us -> 39.3 us  [exchange(): return lax.all_to_all(value, axis, 0, 0, tiled=True)]
    all_to_all x3, waiting for transfers between devices: 9.43 us -> 3.81 us  [exchange(): return lax.all_to_all(value, axis, 0, 0, tiled=True)]
    unnamed x14 -> x22, local copies, waits for them, and re-layouts: 0.04 us -> 3.43 us
    reduce_sum x4 -> x0, other arithmetic: 2.07 us -> none  [the longest x1 1.02 us: local(): totals = jnp.sum(got_g[:, 2 * cells:2 * cells + count].astype(F32), 0)]
  transfers between devices with their start and end apart: 10 -> 12, of which waited for: 8 -> 4; matrix products, arithmetic and copies ran while one was open for 1% -> 2% of each run, Pallas kernels for 4% -> 4%
where the time goes in v3:
time: 123 us; the launch traced here: 122 us
  starting transfers between devices  64.8 us (53%)
  waiting for transfers between devices  33.6 us (27%)
  Pallas kernels  13.1 us (11%)
  local copies, waits for them, and re-layouts  5.68 us (5%)
  other arithmetic  3 us (2%)
    all_to_all x3, starting transfers between devices, exchange(): return lax.all_to_all(value, axis, 0, 0, tiled=True)  39.3 us
    ppermute x4, waiting for transfers between devices, across(): return lax.ppermute(block, ('grp', 'tile'), pairs)  29.8 us
    pallas_call x4, Pallas kernels, on_core(): pl.pallas_call(kernel, out_shape=out_shape, in_specs=[pl.BlockSpec(memory...  13.1 us
    ppermute x4, starting transfers between devices, across(): return lax.ppermute(block, ('grp', 'tile'), pairs)  10.9 us
    ppermute x3, starting transfers between devices, mate(): lax.ppermute(block, 'grp', [(i, i ^ 1) for i in range(lax.axis_size('grp'...  8.78 us
    ppermute x2, starting transfers between devices, shifted(): return lax.ppermute(block, axis, pairs)  5.88 us
    all_to_all x3, waiting for transfers between devices, exchange(): return lax.all_to_all(value, axis, 0, 0, tiled=True)  3.81 us
    unnamed x22, local copies, waits for them, and re-layouts  3.43 us
  transfers between devices with their start and end apart: 12, of which 4 were waited for; matrix products, arithmetic and copies ran while one was open for 2% of the time, Pallas kernels for 4%

profile of v3, /device:TPU:1, one launch (start us, length us, event | category | flops | bytes accessed | tf_op | source)
XLA Modules:
  0.0 122.3 jit_solution(6926785068547770743)
XLA Ops:
  0.7 1.1 convolution_convert_fusion
  2.7 1.2 pad_maximum_fusion
  3.8 19.7 %all-to-all-start = ((bf16[64,72,128]{2,1,0:T(8,128)(2,1)}), bf16[64,72,128]{2,1,0:T(8,128)(2,1)S(1)}, u32[]{:S(2)}, u32[]{:S(2)}) async-start(bf16[64,72,128]{2,1,0:T(8,128)(2,1)} %pad_maximum_fusion), calls=%async_computation | async-start | bytes 2359296 | tf_op jit(solution)/shard_map/all_to_all | solution.py:81
  23.6 3.1 %collective-permute-start.3 = (bf16[8,128,128]{2,1,0:T(8,128)(2,1)S(1)}, bf16[8,128,128]{2,1,0:T(8,128)(2,1)S(1)}, u32[]{:S(2)}, u32[]{:S(2)}) collective-permute-start(bf16[8,128,128]{2,1,0:T(8,128)(2,1)S(1)} %bitcast.40), channel_id=1, source_target_pairs={{64,128},{65,129},{66,130},{67,131},{68,132},{69,133},{70,134},{71... | collective-permute-start | bytes 786440 | tf_op jit(solution)/shard_map/ppermute | solution.py:34
  26.9 1.3 %collective-permute-start.1 = (bf16[264,128]{1,0:T(8,128)(2,1)S(1)}, bf16[264,128]{1,0:T(8,128)(2,1)S(1)}, u32[]{:S(2)}, u32[]{:S(2)}) collective-permute-start(bf16[264,128]{1,0:T(8,128)(2,1)S(1)} %concatenate.36), channel_id=1, source_target_pairs={{1,0},{2,1},{3,2},{4,3},{5,4},{6,5},{7,6},{8,7},{9,8},{10,9},{11,1... | collective-permute-start | bytes 202760 | tf_op jit(solution)/shard_map/ppermute | solution.py:16
  28.2 4.6 %collective-permute-start = (bf16[264,128]{1,0:T(8,128)(2,1)S(1)}, bf16[264,128]{1,0:T(8,128)(2,1)}, u32[]{:S(2)}, u32[]{:S(2)}) collective-permute-start(bf16[264,128]{1,0:T(8,128)(2,1)S(1)} %concatenate.35), channel_id=1, source_target_pairs={{0,1},{1,2},{2,3},{3,4},{4,5},{5,6},{6,7},{7,8},{8,9},{9,10},{10,1... | collective-permute-start | bytes 202760 | tf_op jit(solution)/shard_map/ppermute | solution.py:16
  32.8 3.7 %collective-permute-start.2 = (bf16[2,128,128]{2,1,0:T(8,128)(2,1)S(1)}, bf16[2,128,128]{2,1,0:T(8,128)(2,1)}, u32[]{:S(2)}, u32[]{:S(2)}) collective-permute-start(bf16[2,128,128]{2,1,0:T(8,128)(2,1)S(1)} %get-tuple-element.43), channel_id=1, source_target_pairs={{64,129},{65,130},{66,131},{67,132},{68,133},{69,134},{70,135},{71... | collective-permute-start | bytes 196616 | tf_op jit(solution)/shard_map/ppermute | solution.py:34
  36.6 1.3 %collective-permute-start.4 = (bf16[2,128,128]{2,1,0:T(8,128)(2,1)S(1)}, bf16[2,128,128]{2,1,0:T(8,128)(2,1)}, u32[]{:S(2)}, u32[]{:S(2)}) collective-permute-start(bf16[2,128,128]{2,1,0:T(8,128)(2,1)S(1)} %get-tuple-element.42), channel_id=1, source_target_pairs={{65,128},{66,129},{67,130},{68,131},{69,132},{70,133},{71,134},{72... | collective-permute-start | bytes 196616 | tf_op jit(solution)/shard_map/ppermute | solution.py:34
  37.8 14.3 %collective-permute-done.2 = bf16[2,128,128]{2,1,0:T(8,128)(2,1)} collective-permute-done((bf16[2,128,128]{2,1,0:T(8,128)(2,1)S(1)}, bf16[2,128,128]{2,1,0:T(8,128)(2,1)}, u32[]{:S(2)}, u32[]{:S(2)}) %collective-permute-start.2) | collective-permute-done | bytes 65568 | tf_op jit(solution)/shard_map/ppermute | solution.py:34
  52.1 4.5 %collective-permute-done.4 = bf16[2,128,128]{2,1,0:T(8,128)(2,1)} collective-permute-done((bf16[2,128,128]{2,1,0:T(8,128)(2,1)S(1)}, bf16[2,128,128]{2,1,0:T(8,128)(2,1)}, u32[]{:S(2)}, u32[]{:S(2)}) %collective-permute-start.4) | collective-permute-done | bytes 65568 | tf_op jit(solution)/shard_map/ppermute | solution.py:34
  56.6 4.9 %collective-permute-start.5 = (bf16[64,72,128]{2,1,0:T(8,128)(2,1)S(1)}, bf16[64,72,128]{2,1,0:T(8,128)(2,1)S(1)}, u32[]{:S(2)}, u32[]{:S(2)}) collective-permute-start(bf16[64,72,128]{2,1,0:T(8,128)(2,1)S(1)} %all-to-all-done.got_ref), channel_id=1, source_target_pairs={{0,64},{64,0},{128,192},{192,128},{256,320},{320,256},{384,448},{4... | collective-permute-start | bytes 3538952 | tf_op jit(solution)/shard_map/ppermute | solution.py:20
  62.5 1.9 %collective-permute-start.6 = (bf16[12,128,128]{2,1,0:T(8,128)(2,1)S(1)}, bf16[12,128,128]{2,1,0:T(8,128)(2,1)S(1)}, u32[]{:S(2)}, u32[]{:S(2)}) collective-permute-start(bf16[12,128,128]{2,1,0:T(8,128)(2,1)S(1)} %pad_maximum_fusion.2.wide_ref), channel_id=1, source_target_pairs={{0,64},{64,0},{128,192},{192,128},{256,320},{320,256},{384,448},{4... | collective-permute-start | bytes 1179656 | tf_op jit(solution)/shard_map/ppermute | solution.py:20
  65.3 0.9 pad_maximum_fusion.1.far_ref
  66.5 6.2 %shard_map.93 = (bf16[10,128,128]{2,1,0:T(8,128)(2,1)S(1)}, bf16[64,32,128]{2,1,0:T(8,128)(2,1)}) custom-call(s32[1]{0:T(128)} %bitcast.core_ref, bf16[64,72,128]{2,1,0:T(8,128)(2,1)S(1)} %all-to-all-done.got_ref, bf16[64,72,128]{2,1,0:T(8,128)(2,1)S(1)} %collective-permute-done.5.other_ref, bf16[12,128,128]{2,1,0:T(8,128)(2,1)S(1)} %pad_maximum_fusion.1.far_ref, ...), custom_call_target="tpu_custom_call" | custom-call | flops 200000000 | bytes 12000000 | tf_op jit(solution)/shard_map/pallas_call | solution.py:291
  72.7 9.9 %all-to-all-start.1 = ((bf16[64,32,128]{2,1,0:T(8,128)(2,1)}), bf16[64,32,128]{2,1,0:T(8,128)(2,1)S(1)}, u32[]{:S(2)}, u32[]{:S(2)}) async-start(bf16[64,32,128]{2,1,0:T(8,128)(2,1)} %get-tuple-element.31.sent_ref), calls=%async_computation.1 | async-start | bytes 1048576 | tf_op jit(solution)/shard_map/all_to_all | solution.py:81
  82.6 2.8 %collective-permute-start.7 = (bf16[10,128,128]{2,1,0:T(8,128)(2,1)S(1)}, bf16[10,128,128]{2,1,0:T(8,128)(2,1)S(1)}, u32[]{:S(2)}, u32[]{:S(2)}) collective-permute-start(bf16[10,128,128]{2,1,0:T(8,128)(2,1)S(1)} %get-tuple-element.32.wide_ref), channel_id=1, source_target_pairs={{64,128},{65,129},{66,130},{67,131},{68,132},{69,133},{70,134},{71... | collective-permute-start | bytes 983048 | tf_op jit(solution)/shard_map/ppermute | solution.py:34
  85.4 1.9 %collective-permute-start.8 = (bf16[10,128,128]{2,1,0:T(8,128)(2,1)S(1)}, bf16[10,128,128]{2,1,0:T(8,128)(2,1)S(1)}, u32[]{:S(2)}, u32[]{:S(2)}) collective-permute-start(bf16[10,128,128]{2,1,0:T(8,128)(2,1)S(1)} %get-tuple-element.32.wide_ref), channel_id=1, source_target_pairs={{0,64},{64,0},{128,192},{192,128},{256,320},{320,256},{384,448},{4... | collective-permute-start | bytes 983048 | tf_op jit(solution)/shard_map/ppermute | solution.py:20
  87.6 11.0 %collective-permute-done.7.far_ref = bf16[10,128,128]{2,1,0:T(8,128)(2,1)S(1)} collective-permute-done((bf16[10,128,128]{2,1,0:T(8,128)(2,1)S(1)}, bf16[10,128,128]{2,1,0:T(8,128)(2,1)S(1)}, u32[]{:S(2)}, u32[]{:S(2)}) %collective-permute-start.7) | collective-permute-done | bytes 327712 | tf_op jit(solution)/shard_map/ppermute | solution.py:34
  100.0 1.0 shard_map.95
  101.0 9.6 %all-to-all-start.2 = ((bf16[8,176,128]{2,1,0:T(8,128)(2,1)}), bf16[8,176,128]{2,1,0:T(8,128)(2,1)S(1)}, u32[]{:S(2)}, u32[]{:S(2)}) async-start(bf16[8,176,128]{2,1,0:T(8,128)(2,1)} %shard_map.95), calls=%async_computation.2 | async-start | bytes 720896 | tf_op jit(solution)/shard_map/all_to_all | solution.py:81
  110.7 1.0 copy-done.1
  111.6 1.0 copy-done.3
  112.6 5.2 %shard_map.94 = f32[8,128,128]{2,1,0:T(8,128)} custom-call(s32[1]{0:T(128)} %bitcast.core_ref, bf16[64,72,128]{2,1,0:T(8,128)(2,1)S(1)} %all-to-all-done.got_ref, bf16[64,72,128]{2,1,0:T(8,128)(2,1)S(1)} %collective-permute-done.5.other_ref, bf16[64,32,128]{2,1,0:T(8,128)(2,1)} %get-tuple-element.31.sent_ref, bf16[10,128,128]{2,1,0:T(8,128)(2,1)S(1)} %copy-done.1, ...), custom_call_target="tpu_custom_call" | custom-call | flops 200000000 | bytes 12000000 | tf_op jit(solution)/shard_map/pallas_call | solution.py:291
  117.8 3.8 %all-to-all-done.2.last_ref = bf16[8,176,128]{2,1,0:T(8,128)(2,1)S(1)} async-done(((bf16[8,176,128]{2,1,0:T(8,128)(2,1)}), bf16[8,176,128]{2,1,0:T(8,128)(2,1)S(1)}, u32[]{:S(2)}, u32[]{:S(2)}) %all-to-all-start.2) | async-done | bytes 360480 | tf_op jit(solution)/shard_map/all_to_all | solution.py:81
  (53 shorter events, 5.4 us)
Async XLA Ops:
  0.6 1.8 %copy-start.7 = (bf16[64,256]{1,0:T(8,128)(2,1)S(1)}, bf16[64,256]{1,0:T(8,128)(2,1)}, u32[]{:S(2)}) copy-start(bf16[64,256]{1,0:T(8,128)(2,1)} %param.8) | copy-start | bytes 98308
  3.8 19.8 %copy-start.5 = (bf16[1,8,128,128]{3,2,1,0:T(8,128)(2,1)S(1)}, bf16[1,8,128,128]{3,2,1,0:T(8,128)(2,1)}, u32[]{:S(2)}) copy-start(bf16[1,8,128,128]{3,2,1,0:T(8,128)(2,1)} %param.6) | copy-start | bytes 786436
  3.8 23.0 %copy-start.8 = (f32[1,8,128]{2,1,0:T(8,128)S(1)}, f32[1,8,128]{2,1,0:T(8,128)}, u32[]{:S(2)}) copy-start(f32[1,8,128]{2,1,0:T(8,128)} %param.7) | copy-start | bytes 12292
  3.8 52.8 %all-to-all-start = ((bf16[64,72,128]{2,1,0:T(8,128)(2,1)}), bf16[64,72,128]{2,1,0:T(8,128)(2,1)S(1)}, u32[]{:S(2)}, u32[]{:S(2)}) async-start(bf16[64,72,128]{2,1,0:T(8,128)(2,1)} %pad_maximum_fusion), calls=%async_computation | async-start | bytes 2359296 | tf_op jit(solution)/shard_map/all_to_all | solution.py:81
  23.6 40.9 %copy-start.9 = (f32[9,128]{1,0:T(8,128)S(1)}, f32[9,128]{1,0:T(8,128)}, u32[]{:S(2)}) copy-start(f32[9,128]{1,0:T(8,128)} %param.9) | copy-start | bytes 13828
  23.6 40.9 %copy-start.10 = (f32[128]{0:T(128)S(1)}, f32[128]{0:T(128)}, u32[]{:S(2)}) copy-start(f32[128]{0:T(128)} %param.10) | copy-start | bytes 1540
  23.6 33.0 %collective-permute-start.3 = (bf16[8,128,128]{2,1,0:T(8,128)(2,1)S(1)}, bf16[8,128,128]{2,1,0:T(8,128)(2,1)S(1)}, u32[]{:S(2)}, u32[]{:S(2)}) collective-permute-start(bf16[8,128,128]{2,1,0:T(8,128)(2,1)S(1)} %bitcast.40), channel_id=1, source_target_pairs={{64,128},{65,129},{66,130},{67,131},{68,132},{69,133},{70,134},{71... | collective-permute-start | bytes 786440 | tf_op jit(solution)/shard_map/ppermute | solution.py:34
  26.9 29.7 %collective-permute-start.1 = (bf16[264,128]{1,0:T(8,128)(2,1)S(1)}, bf16[264,128]{1,0:T(8,128)(2,1)S(1)}, u32[]{:S(2)}, u32[]{:S(2)}) collective-permute-start(bf16[264,128]{1,0:T(8,128)(2,1)S(1)} %concatenate.36), channel_id=1, source_target_pairs={{1,0},{2,1},{3,2},{4,3},{5,4},{6,5},{7,6},{8,7},{9,8},{10,9},{11,1... | collective-permute-start | bytes 202760 | tf_op jit(solution)/shard_map/ppermute | solution.py:16
  28.2 28.4 %collective-permute-start = (bf16[264,128]{1,0:T(8,128)(2,1)S(1)}, bf16[264,128]{1,0:T(8,128)(2,1)}, u32[]{:S(2)}, u32[]{:S(2)}) collective-permute-start(bf16[264,128]{1,0:T(8,128)(2,1)S(1)} %concatenate.35), channel_id=1, source_target_pairs={{0,1},{1,2},{2,3},{3,4},{4,5},{5,6},{6,7},{7,8},{8,9},{9,10},{10,1... | collective-permute-start | bytes 202760 | tf_op jit(solution)/shard_map/ppermute | solution.py:16
  32.8 19.3 %collective-permute-start.2 = (bf16[2,128,128]{2,1,0:T(8,128)(2,1)S(1)}, bf16[2,128,128]{2,1,0:T(8,128)(2,1)}, u32[]{:S(2)}, u32[]{:S(2)}) collective-permute-start(bf16[2,128,128]{2,1,0:T(8,128)(2,1)S(1)} %get-tuple-element.43), channel_id=1, source_target_pairs={{64,129},{65,130},{66,131},{67,132},{68,133},{69,134},{70,135},{71... | collective-permute-start | bytes 196616 | tf_op jit(solution)/shard_map/ppermute | solution.py:34
  36.6 20.1 %collective-permute-start.4 = (bf16[2,128,128]{2,1,0:T(8,128)(2,1)S(1)}, bf16[2,128,128]{2,1,0:T(8,128)(2,1)}, u32[]{:S(2)}, u32[]{:S(2)}) collective-permute-start(bf16[2,128,128]{2,1,0:T(8,128)(2,1)S(1)} %get-tuple-element.42), channel_id=1, source_target_pairs={{65,128},{66,129},{67,130},{68,131},{69,132},{70,133},{71,134},{72... | collective-permute-start | bytes 196616 | tf_op jit(solution)/shard_map/ppermute | solution.py:34
  56.6 5.8 %copy-start.6 = (bf16[264,128]{1,0:T(8,128)(2,1)}, bf16[264,128]{1,0:T(8,128)(2,1)S(1)}, u32[]{:S(2)}) copy-start(bf16[264,128]{1,0:T(8,128)(2,1)S(1)} %collective-permute-done.1) | copy-start | bytes 202756
  56.6 9.6 %collective-permute-start.5 = (bf16[64,72,128]{2,1,0:T(8,128)(2,1)S(1)}, bf16[64,72,128]{2,1,0:T(8,128)(2,1)S(1)}, u32[]{:S(2)}, u32[]{:S(2)}) collective-permute-start(bf16[64,72,128]{2,1,0:T(8,128)(2,1)S(1)} %all-to-all-done.got_ref), channel_id=1, source_target_pairs={{0,64},{64,0},{128,192},{192,128},{256,320},{320,256},{384,448},{4... | collective-permute-start | bytes 3538952 | tf_op jit(solution)/shard_map/ppermute | solution.py:20
  62.4 4.1 %copy-start.4 = (bf16[128,128]{1,0:T(8,128)(2,1)S(1)}, bf16[128,128]{1,0:T(8,128)(2,1)}, u32[]{:S(2)}) copy-start(bf16[128,128]{1,0:T(8,128)(2,1)} %constant.32.clone.table_ref) | copy-start | bytes 98308
  62.5 3.7 %collective-permute-start.6 = (bf16[12,128,128]{2,1,0:T(8,128)(2,1)S(1)}, bf16[12,128,128]{2,1,0:T(8,128)(2,1)S(1)}, u32[]{:S(2)}, u32[]{:S(2)}) collective-permute-start(bf16[12,128,128]{2,1,0:T(8,128)(2,1)S(1)} %pad_maximum_fusion.2.wide_ref), channel_id=1, source_target_pairs={{0,64},{64,0},{128,192},{192,128},{256,320},{320,256},{384,448},{4... | collective-permute-start | bytes 1179656 | tf_op jit(solution)/shard_map/ppermute | solution.py:20
  72.7 27.3 %all-to-all-start.1 = ((bf16[64,32,128]{2,1,0:T(8,128)(2,1)}), bf16[64,32,128]{2,1,0:T(8,128)(2,1)S(1)}, u32[]{:S(2)}, u32[]{:S(2)}) async-start(bf16[64,32,128]{2,1,0:T(8,128)(2,1)} %get-tuple-element.31.sent_ref), calls=%async_computation.1 | async-start | bytes 1048576 | tf_op jit(solution)/shard_map/all_to_all | solution.py:81
  82.6 15.9 %collective-permute-start.7 = (bf16[10,128,128]{2,1,0:T(8,128)(2,1)S(1)}, bf16[10,128,128]{2,1,0:T(8,128)(2,1)S(1)}, u32[]{:S(2)}, u32[]{:S(2)}) collective-permute-start(bf16[10,128,128]{2,1,0:T(8,128)(2,1)S(1)} %get-tuple-element.32.wide_ref), channel_id=1, source_target_pairs={{64,128},{65,129},{66,130},{67,131},{68,132},{69,133},{70,134},{71... | collective-permute-start | bytes 983048 | tf_op jit(solution)/shard_map/ppermute | solution.py:34
  85.4 13.9 %collective-permute-start.8 = (bf16[10,128,128]{2,1,0:T(8,128)(2,1)S(1)}, bf16[10,128,128]{2,1,0:T(8,128)(2,1)S(1)}, u32[]{:S(2)}, u32[]{:S(2)}) collective-permute-start(bf16[10,128,128]{2,1,0:T(8,128)(2,1)S(1)} %get-tuple-element.32.wide_ref), channel_id=1, source_target_pairs={{0,64},{64,0},{128,192},{192,128},{256,320},{320,256},{384,448},{4... | collective-permute-start | bytes 983048 | tf_op jit(solution)/shard_map/ppermute | solution.py:20
  98.6 0.7 copy-start
  99.3 0.7 copy-start.2
  101.0 20.6 %all-to-all-start.2 = ((bf16[8,176,128]{2,1,0:T(8,128)(2,1)}), bf16[8,176,128]{2,1,0:T(8,128)(2,1)S(1)}, u32[]{:S(2)}, u32[]{:S(2)}) async-start(bf16[8,176,128]{2,1,0:T(8,128)(2,1)} %shard_map.95), calls=%async_computation.2 | async-start | bytes 720896 | tf_op jit(solution)/shard_map/all_to_all | solution.py:81
  110.7 1.0 copy-start.1
  111.6 1.0 copy-start.3

commit v4 on v3

--- a/solution.py
+++ b/solution.py
@@ -35,14 +35,14 @@
 
 
 def edge_pack(columns, cot):
-    flat = columns.reshape(-1, columns.shape[-1])
-    return jnp.concatenate([flat, cot, jnp.zeros((5, flat.shape[1]), BF)], 0)
-
-
-def edge_unpack(packed, bins):
-    columns = packed[: 2 * bins].reshape(2, bins, -1)
-    cot = packed[2 * bins : 2 * bins + 3].astype(F32).sum(0)
-    return columns, cot[None]
+    bins = columns.shape[1]
+    extra = jnp.pad(cot, ((0, bins - cot.shape[0]), (0, 0)))
+    return jnp.concatenate([columns, extra[None]], 0)
+
+
+def edge_unpack(packed):
+    cot = packed[2, :3].astype(F32).sum(0)
+    return packed[:2], cot[None]
 
 
 def to_spec(forward_tab, block):
@@ -344,8 +344,8 @@
     far = [across(tail, 1), across(hidden[0], 0), across(head, -1)]
     got, low_t, high_t, far = tied(got, low_t, high_t, far)
     far = jnp.concatenate(far, 0)
-    low_cols, low_cot = edge_unpack(low_t, bins)
-    high_cols, high_cot = edge_unpack(high_t, bins)
+    low_cols, low_cot = edge_unpack(low_t)
+    high_cols, high_cot = edge_unpack(high_t)
     wide = jnp.concatenate([low_cols, hidden[0], high_cols], 0)
     cot_wide = jnp.concatenate([low_cot, cotangent[0], high_cot], 0)
     cot_lanes = jnp.broadcast_to(cot_wide[:, :, None], (near, bins, chans))

time: 123 us -> 123 us (level)
    all_to_all x3, starting transfers between devices: 39.3 us -> 38 us  [exchange(): return lax.all_to_all(value, axis, 0, 0, tiled=True)]
where the time goes in v4:
time: 123 us; the launch traced here: 122 us
  starting transfers between devices  64.6 us (53%)
  waiting for transfers between devices  33.7 us (27%)
  Pallas kernels  13.1 us (11%)
  local copies, waits for them, and re-layouts  5.55 us (5%)
  other arithmetic  3.04 us (2%)
    all_to_all x3, starting transfers between devices, exchange(): return lax.all_to_all(value, axis, 0, 0, tiled=True)  38 us
    ppermute x4, waiting for transfers between devices, across(): return lax.ppermute(block, ('grp', 'tile'), pairs)  29.9 us
    pallas_call x4, Pallas kernels, on_core(): pl.pallas_call(kernel, out_shape=out_shape, in_specs=[pl.BlockSpec(memory...  13.1 us
    ppermute x4, starting transfers between devices, across(): return lax.ppermute(block, ('grp', 'tile'), pairs)  11.7 us
    ppermute x3, starting transfers between devices, mate(): lax.ppermute(block, 'grp', [(i, i ^ 1) for i in range(lax.axis_size('grp'...  8.7 us
    ppermute x2, starting transfers between devices, shifted(): return lax.ppermute(block, axis, pairs)  6.2 us
    all_to_all x3, waiting for transfers between devices, exchange(): return lax.all_to_all(value, axis, 0, 0, tiled=True)  3.81 us
    unnamed x22, local copies, waits for them, and re-layouts  3.43 us
  transfers between devices with their start and end apart: 12, of which 4 were waited for; matrix products, arithmetic and copies ran while one was open for 2% of the time, Pallas kernels for 4%

profile of v4, /device:TPU:1, one launch (start us, length us, event | category | flops | bytes accessed | tf_op | source)
XLA Modules:
  0.0 122.2 jit_solution(7539996600442112201)
XLA Ops:
  0.7 1.1 convolution_convert_fusion
  2.7 1.2 pad_maximum_fusion
  3.8 19.7 %all-to-all-start = ((bf16[64,72,128]{2,1,0:T(8,128)(2,1)}), bf16[64,72,128]{2,1,0:T(8,128)(2,1)S(1)}, u32[]{:S(2)}, u32[]{:S(2)}) async-start(bf16[64,72,128]{2,1,0:T(8,128)(2,1)} %pad_maximum_fusion), calls=%async_computation | async-start | bytes 2359296 | tf_op jit(solution)/shard_map/all_to_all | solution.py:81
  23.7 1.3 %collective-permute-start.1 = (bf16[3,128,128]{2,1,0:T(8,128)(2,1)S(1)}, bf16[3,128,128]{2,1,0:T(8,128)(2,1)S(1)}, u32[]{:S(2)}, u32[]{:S(2)}) collective-permute-start(bf16[3,128,128]{2,1,0:T(8,128)(2,1)S(1)} %pad_maximum_fusion.4), channel_id=1, source_target_pairs={{1,0},{2,1},{3,2},{4,3},{5,4},{6,5},{7,6},{8,7},{9,8},{10,9},{11,1... | collective-permute-start | bytes 294920 | tf_op jit(solution)/shard_map/ppermute | solution.py:16
  25.0 3.1 %collective-permute-start.3 = (bf16[8,128,128]{2,1,0:T(8,128)(2,1)S(1)}, bf16[8,128,128]{2,1,0:T(8,128)(2,1)S(1)}, u32[]{:S(2)}, u32[]{:S(2)}) collective-permute-start(bf16[8,128,128]{2,1,0:T(8,128)(2,1)S(1)} %bitcast.40), channel_id=1, source_target_pairs={{64,128},{65,129},{66,130},{67,131},{68,132},{69,133},{70,134},{71... | collective-permute-start | bytes 786440 | tf_op jit(solution)/shard_map/ppermute | solution.py:34
  28.2 4.9 %collective-permute-start = (bf16[3,128,128]{2,1,0:T(8,128)(2,1)S(1)}, bf16[3,128,128]{2,1,0:T(8,128)(2,1)}, u32[]{:S(2)}, u32[]{:S(2)}) collective-permute-start(bf16[3,128,128]{2,1,0:T(8,128)(2,1)S(1)} %pad_maximum_fusion.3), channel_id=1, source_target_pairs={{0,1},{1,2},{2,3},{3,4},{4,5},{5,6},{6,7},{7,8},{8,9},{9,10},{10,1... | collective-permute-start | bytes 294920 | tf_op jit(solution)/shard_map/ppermute | solution.py:16
  33.1 3.2 %collective-permute-start.2 = (bf16[2,128,128]{2,1,0:T(8,128)(2,1)S(1)}, bf16[2,128,128]{2,1,0:T(8,128)(2,1)}, u32[]{:S(2)}, u32[]{:S(2)}) collective-permute-start(bf16[2,128,128]{2,1,0:T(8,128)(2,1)S(1)} %get-tuple-element.43), channel_id=1, source_target_pairs={{64,129},{65,130},{66,131},{67,132},{68,133},{69,134},{70,135},{71... | collective-permute-start | bytes 196616 | tf_op jit(solution)/shard_map/ppermute | solution.py:34
  36.3 1.3 %collective-permute-start.4 = (bf16[2,128,128]{2,1,0:T(8,128)(2,1)S(1)}, bf16[2,128,128]{2,1,0:T(8,128)(2,1)}, u32[]{:S(2)}, u32[]{:S(2)}) collective-permute-start(bf16[2,128,128]{2,1,0:T(8,128)(2,1)S(1)} %get-tuple-element.42), channel_id=1, source_target_pairs={{65,128},{66,129},{67,130},{68,131},{69,132},{70,133},{71,134},{72... | collective-permute-start | bytes 196616 | tf_op jit(solution)/shard_map/ppermute | solution.py:34
  37.6 14.7 %collective-permute-done.2 = bf16[2,128,128]{2,1,0:T(8,128)(2,1)} collective-permute-done((bf16[2,128,128]{2,1,0:T(8,128)(2,1)S(1)}, bf16[2,128,128]{2,1,0:T(8,128)(2,1)}, u32[]{:S(2)}, u32[]{:S(2)}) %collective-permute-start.2) | collective-permute-done | bytes 65568 | tf_op jit(solution)/shard_map/ppermute | solution.py:34
  52.3 4.3 %collective-permute-done.4 = bf16[2,128,128]{2,1,0:T(8,128)(2,1)} collective-permute-done((bf16[2,128,128]{2,1,0:T(8,128)(2,1)S(1)}, bf16[2,128,128]{2,1,0:T(8,128)(2,1)}, u32[]{:S(2)}, u32[]{:S(2)}) %collective-permute-start.4) | collective-permute-done | bytes 65568 | tf_op jit(solution)/shard_map/ppermute | solution.py:34
  56.6 4.9 %collective-permute-start.5 = (bf16[64,72,128]{2,1,0:T(8,128)(2,1)S(1)}, bf16[64,72,128]{2,1,0:T(8,128)(2,1)S(1)}, u32[]{:S(2)}, u32[]{:S(2)}) collective-permute-start(bf16[64,72,128]{2,1,0:T(8,128)(2,1)S(1)} %all-to-all-done.got_ref), channel_id=1, source_target_pairs={{0,64},{64,0},{128,192},{192,128},{256,320},{320,256},{384,448},{4... | collective-permute-start | bytes 3538952 | tf_op jit(solution)/shard_map/ppermute | solution.py:20
  62.4 1.9 %collective-permute-start.6 = (bf16[12,128,128]{2,1,0:T(8,128)(2,1)S(1)}, bf16[12,128,128]{2,1,0:T(8,128)(2,1)S(1)}, u32[]{:S(2)}, u32[]{:S(2)}) collective-permute-start(bf16[12,128,128]{2,1,0:T(8,128)(2,1)S(1)} %pad_maximum_fusion.2.wide_ref), channel_id=1, source_target_pairs={{0,64},{64,0},{128,192},{192,128},{256,320},{320,256},{384,448},{4... | collective-permute-start | bytes 1179656 | tf_op jit(solution)/shard_map/ppermute | solution.py:20
  65.2 0.9 pad_maximum_fusion.1.far_ref
  66.4 6.2 %shard_map.93 = (bf16[10,128,128]{2,1,0:T(8,128)(2,1)S(1)}, bf16[64,32,128]{2,1,0:T(8,128)(2,1)}) custom-call(s32[1]{0:T(128)} %bitcast.core_ref, bf16[64,72,128]{2,1,0:T(8,128)(2,1)S(1)} %all-to-all-done.got_ref, bf16[64,72,128]{2,1,0:T(8,128)(2,1)S(1)} %collective-permute-done.5.other_ref, bf16[12,128,128]{2,1,0:T(8,128)(2,1)S(1)} %pad_maximum_fusion.1.far_ref, ...), custom_call_target="tpu_custom_call" | custom-call | flops 200000000 | bytes 12000000 | tf_op jit(solution)/shard_map/pallas_call | solution.py:291
  72.6 10.0 %all-to-all-start.1 = ((bf16[64,32,128]{2,1,0:T(8,128)(2,1)}), bf16[64,32,128]{2,1,0:T(8,128)(2,1)S(1)}, u32[]{:S(2)}, u32[]{:S(2)}) async-start(bf16[64,32,128]{2,1,0:T(8,128)(2,1)} %get-tuple-element.31.sent_ref), calls=%async_computation.1 | async-start | bytes 1048576 | tf_op jit(solution)/shard_map/all_to_all | solution.py:81
  82.6 4.1 %collective-permute-start.7 = (bf16[10,128,128]{2,1,0:T(8,128)(2,1)S(1)}, bf16[10,128,128]{2,1,0:T(8,128)(2,1)S(1)}, u32[]{:S(2)}, u32[]{:S(2)}) collective-permute-start(bf16[10,128,128]{2,1,0:T(8,128)(2,1)S(1)} %get-tuple-element.32.wide_ref), channel_id=1, source_target_pairs={{64,128},{65,129},{66,130},{67,131},{68,132},{69,133},{70,134},{71... | collective-permute-start | bytes 983048 | tf_op jit(solution)/shard_map/ppermute | solution.py:34
  86.7 1.9 %collective-permute-start.8 = (bf16[10,128,128]{2,1,0:T(8,128)(2,1)S(1)}, bf16[10,128,128]{2,1,0:T(8,128)(2,1)S(1)}, u32[]{:S(2)}, u32[]{:S(2)}) collective-permute-start(bf16[10,128,128]{2,1,0:T(8,128)(2,1)S(1)} %get-tuple-element.32.wide_ref), channel_id=1, source_target_pairs={{0,64},{64,0},{128,192},{192,128},{256,320},{320,256},{384,448},{4... | collective-permute-start | bytes 983048 | tf_op jit(solution)/shard_map/ppermute | solution.py:20
  88.9 10.9 %collective-permute-done.7.far_ref = bf16[10,128,128]{2,1,0:T(8,128)(2,1)S(1)} collective-permute-done((bf16[10,128,128]{2,1,0:T(8,128)(2,1)S(1)}, bf16[10,128,128]{2,1,0:T(8,128)(2,1)S(1)}, u32[]{:S(2)}, u32[]{:S(2)}) %collective-permute-start.7) | collective-permute-done | bytes 327712 | tf_op jit(solution)/shard_map/ppermute | solution.py:34
  101.2 1.0 shard_map.95
  102.2 8.3 %all-to-all-start.2 = ((bf16[8,176,128]{2,1,0:T(8,128)(2,1)}), bf16[8,176,128]{2,1,0:T(8,128)(2,1)S(1)}, u32[]{:S(2)}, u32[]{:S(2)}) async-start(bf16[8,176,128]{2,1,0:T(8,128)(2,1)} %shard_map.95), calls=%async_computation.2 | async-start | bytes 720896 | tf_op jit(solution)/shard_map/all_to_all | solution.py:81
  110.5 1.0 copy-done.1
  111.5 1.0 copy-done.3
  112.5 5.2 %shard_map.94 = f32[8,128,128]{2,1,0:T(8,128)} custom-call(s32[1]{0:T(128)} %bitcast.core_ref, bf16[64,72,128]{2,1,0:T(8,128)(2,1)S(1)} %all-to-all-done.got_ref, bf16[64,72,128]{2,1,0:T(8,128)(2,1)S(1)} %collective-permute-done.5.other_ref, bf16[64,32,128]{2,1,0:T(8,128)(2,1)} %get-tuple-element.31.sent_ref, bf16[10,128,128]{2,1,0:T(8,128)(2,1)S(1)} %copy-done.1, ...), custom_call_target="tpu_custom_call" | custom-call | flops 200000000 | bytes 12000000 | tf_op jit(solution)/shard_map/pallas_call | solution.py:291
  117.7 3.8 %all-to-all-done.2.last_ref = bf16[8,176,128]{2,1,0:T(8,128)(2,1)S(1)} async-done(((bf16[8,176,128]{2,1,0:T(8,128)(2,1)}), bf16[8,176,128]{2,1,0:T(8,128)(2,1)S(1)}, u32[]{:S(2)}, u32[]{:S(2)}) %all-to-all-start.2) | async-done | bytes 360480 | tf_op jit(solution)/shard_map/all_to_all | solution.py:81
  (54 shorter events, 5.3 us)
Async XLA Ops:
  0.6 1.8 %copy-start.7 = (bf16[64,256]{1,0:T(8,128)(2,1)S(1)}, bf16[64,256]{1,0:T(8,128)(2,1)}, u32[]{:S(2)}) copy-start(bf16[64,256]{1,0:T(8,128)(2,1)} %param.8) | copy-start | bytes 98308
  3.8 19.7 %copy-start.8 = (f32[1,8,128]{2,1,0:T(8,128)S(1)}, f32[1,8,128]{2,1,0:T(8,128)}, u32[]{:S(2)}) copy-start(f32[1,8,128]{2,1,0:T(8,128)} %param.7) | copy-start | bytes 12292
  3.8 19.8 %copy-start.5 = (bf16[1,8,128,128]{3,2,1,0:T(8,128)(2,1)S(1)}, bf16[1,8,128,128]{3,2,1,0:T(8,128)(2,1)}, u32[]{:S(2)}) copy-start(bf16[1,8,128,128]{3,2,1,0:T(8,128)(2,1)} %param.6) | copy-start | bytes 786436
  3.8 52.8 %all-to-all-start = ((bf16[64,72,128]{2,1,0:T(8,128)(2,1)}), bf16[64,72,128]{2,1,0:T(8,128)(2,1)S(1)}, u32[]{:S(2)}, u32[]{:S(2)}) async-start(bf16[64,72,128]{2,1,0:T(8,128)(2,1)} %pad_maximum_fusion), calls=%async_computation | async-start | bytes 2359296 | tf_op jit(solution)/shard_map/all_to_all | solution.py:81
  23.6 40.8 %copy-start.9 = (f32[9,128]{1,0:T(8,128)S(1)}, f32[9,128]{1,0:T(8,128)}, u32[]{:S(2)}) copy-start(f32[9,128]{1,0:T(8,128)} %param.9) | copy-start | bytes 13828
  23.6 40.8 %copy-start.10 = (f32[128]{0:T(128)S(1)}, f32[128]{0:T(128)}, u32[]{:S(2)}) copy-start(f32[128]{0:T(128)} %param.10) | copy-start | bytes 1540
  23.7 32.9 %collective-permute-start.1 = (bf16[3,128,128]{2,1,0:T(8,128)(2,1)S(1)}, bf16[3,128,128]{2,1,0:T(8,128)(2,1)S(1)}, u32[]{:S(2)}, u32[]{:S(2)}) collective-permute-start(bf16[3,128,128]{2,1,0:T(8,128)(2,1)S(1)} %pad_maximum_fusion.4), channel_id=1, source_target_pairs={{1,0},{2,1},{3,2},{4,3},{5,4},{6,5},{7,6},{8,7},{9,8},{10,9},{11,1... | collective-permute-start | bytes 294920 | tf_op jit(solution)/shard_map/ppermute | solution.py:16
  25.0 31.6 %collective-permute-start.3 = (bf16[8,128,128]{2,1,0:T(8,128)(2,1)S(1)}, bf16[8,128,128]{2,1,0:T(8,128)(2,1)S(1)}, u32[]{:S(2)}, u32[]{:S(2)}) collective-permute-start(bf16[8,128,128]{2,1,0:T(8,128)(2,1)S(1)} %bitcast.40), channel_id=1, source_target_pairs={{64,128},{65,129},{66,130},{67,131},{68,132},{69,133},{70,134},{71... | collective-permute-start | bytes 786440 | tf_op jit(solution)/shard_map/ppermute | solution.py:34
  28.2 28.4 %collective-permute-start = (bf16[3,128,128]{2,1,0:T(8,128)(2,1)S(1)}, bf16[3,128,128]{2,1,0:T(8,128)(2,1)}, u32[]{:S(2)}, u32[]{:S(2)}) collective-permute-start(bf16[3,128,128]{2,1,0:T(8,128)(2,1)S(1)} %pad_maximum_fusion.3), channel_id=1, source_target_pairs={{0,1},{1,2},{2,3},{3,4},{4,5},{5,6},{6,7},{7,8},{8,9},{9,10},{10,1... | collective-permute-start | bytes 294920 | tf_op jit(solution)/shard_map/ppermute | solution.py:16
  33.1 19.2 %collective-permute-start.2 = (bf16[2,128,128]{2,1,0:T(8,128)(2,1)S(1)}, bf16[2,128,128]{2,1,0:T(8,128)(2,1)}, u32[]{:S(2)}, u32[]{:S(2)}) collective-permute-start(bf16[2,128,128]{2,1,0:T(8,128)(2,1)S(1)} %get-tuple-element.43), channel_id=1, source_target_pairs={{64,129},{65,130},{66,131},{67,132},{68,133},{69,134},{70,135},{71... | collective-permute-start | bytes 196616 | tf_op jit(solution)/shard_map/ppermute | solution.py:34
  36.3 20.3 %collective-permute-start.4 = (bf16[2,128,128]{2,1,0:T(8,128)(2,1)S(1)}, bf16[2,128,128]{2,1,0:T(8,128)(2,1)}, u32[]{:S(2)}, u32[]{:S(2)}) collective-permute-start(bf16[2,128,128]{2,1,0:T(8,128)(2,1)S(1)} %get-tuple-element.42), channel_id=1, source_target_pairs={{65,128},{66,129},{67,130},{68,131},{69,132},{70,133},{71,134},{72... | collective-permute-start | bytes 196616 | tf_op jit(solution)/shard_map/ppermute | solution.py:34
  56.6 5.8 %copy-start.6 = (bf16[3,128,128]{2,1,0:T(8,128)(2,1)}, bf16[3,128,128]{2,1,0:T(8,128)(2,1)S(1)}, u32[]{:S(2)}) copy-start(bf16[3,128,128]{2,1,0:T(8,128)(2,1)S(1)} %collective-permute-done.1) | copy-start | bytes 294916
  56.6 9.5 %collective-permute-start.5 = (bf16[64,72,128]{2,1,0:T(8,128)(2,1)S(1)}, bf16[64,72,128]{2,1,0:T(8,128)(2,1)S(1)}, u32[]{:S(2)}, u32[]{:S(2)}) collective-permute-start(bf16[64,72,128]{2,1,0:T(8,128)(2,1)S(1)} %all-to-all-done.got_ref), channel_id=1, source_target_pairs={{0,64},{64,0},{128,192},{192,128},{256,320},{320,256},{384,448},{4... | collective-permute-start | bytes 3538952 | tf_op jit(solution)/shard_map/ppermute | solution.py:20
  62.4 4.1 %copy-start.4 = (bf16[128,128]{1,0:T(8,128)(2,1)S(1)}, bf16[128,128]{1,0:T(8,128)(2,1)}, u32[]{:S(2)}) copy-start(bf16[128,128]{1,0:T(8,128)(2,1)} %constant.32.clone.table_ref) | copy-start | bytes 98308
  62.4 3.7 %collective-permute-start.6 = (bf16[12,128,128]{2,1,0:T(8,128)(2,1)S(1)}, bf16[12,128,128]{2,1,0:T(8,128)(2,1)S(1)}, u32[]{:S(2)}, u32[]{:S(2)}) collective-permute-start(bf16[12,128,128]{2,1,0:T(8,128)(2,1)S(1)} %pad_maximum_fusion.2.wide_ref), channel_id=1, source_target_pairs={{0,64},{64,0},{128,192},{192,128},{256,320},{320,256},{384,448},{4... | collective-permute-start | bytes 1179656 | tf_op jit(solution)/shard_map/ppermute | solution.py:20
  72.6 28.6 %all-to-all-start.1 = ((bf16[64,32,128]{2,1,0:T(8,128)(2,1)}), bf16[64,32,128]{2,1,0:T(8,128)(2,1)S(1)}, u32[]{:S(2)}, u32[]{:S(2)}) async-start(bf16[64,32,128]{2,1,0:T(8,128)(2,1)} %get-tuple-element.31.sent_ref), calls=%async_computation.1 | async-start | bytes 1048576 | tf_op jit(solution)/shard_map/all_to_all | solution.py:81
  82.6 17.1 %collective-permute-start.7 = (bf16[10,128,128]{2,1,0:T(8,128)(2,1)S(1)}, bf16[10,128,128]{2,1,0:T(8,128)(2,1)S(1)}, u32[]{:S(2)}, u32[]{:S(2)}) collective-permute-start(bf16[10,128,128]{2,1,0:T(8,128)(2,1)S(1)} %get-tuple-element.32.wide_ref), channel_id=1, source_target_pairs={{64,128},{65,129},{66,130},{67,131},{68,132},{69,133},{70,134},{71... | collective-permute-start | bytes 983048 | tf_op jit(solution)/shard_map/ppermute | solution.py:34
  86.7 13.8 %collective-permute-start.8 = (bf16[10,128,128]{2,1,0:T(8,128)(2,1)S(1)}, bf16[10,128,128]{2,1,0:T(8,128)(2,1)S(1)}, u32[]{:S(2)}, u32[]{:S(2)}) collective-permute-start(bf16[10,128,128]{2,1,0:T(8,128)(2,1)S(1)} %get-tuple-element.32.wide_ref), channel_id=1, source_target_pairs={{0,64},{64,0},{128,192},{192,128},{256,320},{320,256},{384,448},{4... | collective-permute-start | bytes 983048 | tf_op jit(solution)/shard_map/ppermute | solution.py:20
  99.8 0.7 copy-start
  100.5 0.7 copy-start.2
  102.2 19.3 %all-to-all-start.2 = ((bf16[8,176,128]{2,1,0:T(8,128)(2,1)}), bf16[8,176,128]{2,1,0:T(8,128)(2,1)S(1)}, u32[]{:S(2)}, u32[]{:S(2)}) async-start(bf16[8,176,128]{2,1,0:T(8,128)(2,1)} %shard_map.95), calls=%async_computation.2 | async-start | bytes 720896 | tf_op jit(solution)/shard_map/all_to_all | solution.py:81
  110.5 1.0 copy-start.1
  111.5 1.0 copy-start.3

commit v5 on v4

--- a/solution.py
+++ b/solution.py
@@ -34,15 +34,8 @@
     return lax.ppermute(block, ("grp", "tile"), pairs)
 
 
-def edge_pack(columns, cot):
-    bins = columns.shape[1]
-    extra = jnp.pad(cot, ((0, bins - cot.shape[0]), (0, 0)))
-    return jnp.concatenate([columns, extra[None]], 0)
-
-
-def edge_unpack(packed):
-    cot = packed[2, :3].astype(F32).sum(0)
-    return packed[:2], cot[None]
+def edge_pack(cot, bins):
+    return jnp.pad(cot, ((0, bins - cot.shape[0]), (0, 0)))[None]
 
 
 def to_spec(forward_tab, block):
@@ -113,6 +106,7 @@
     mix_ref,
     turn_ref,
     sum_ref,
+    edge_ref,
 ):
     modes = table_ref.shape[0] // 4
     forward_tab = table_ref[: 2 * modes, :]
@@ -125,10 +119,13 @@
     band = 32
     core = core_ref[0]
     sum_ref[...] = jnp.zeros_like(sum_ref)
+    for edge, column in enumerate((0, near + 3)):
+        cot = jnp.sum(wide_ref[column, 0:16, :].astype(F32), 0, keepdims=True)
+        edge_ref[edge] = jnp.broadcast_to(cot, (chans, bins)).T
     spec_ref[:, near:, :] = jnp.zeros((2 * modes, rows - near, chans), F32)
     for cell in range(near):
         spec_ref[:, cell, :] = jnp.dot(
-            forward_tab, wide_ref[cell + 1], preferred_element_type=F32
+            forward_tab, wide_ref[cell + 2], preferred_element_type=F32
         )
 
     def mix_one(mode, carry):
@@ -147,7 +144,7 @@
 
     lax.fori_loop(0, modes, mix_one, 0, unroll=4)
 
-    def one_cell(cell, own):
+    def one_cell(cell, own, scale_ref, place):
         spectral = jnp.dot(inverse_tab, mix_ref[cell].astype(BF), preferred_element_type=F32)
         pieces = []
         for start in range(0, bins, band):
@@ -155,12 +152,13 @@
             total = spectral[span]
             windows = []
             for row, ref in enumerate((far_ref, wide_ref, close_ref)):
+                skip = 1 if row else 0
                 for col in range(3):
-                    window = ref[cell + col, span, :].astype(F32)
+                    window = ref[cell + col + skip, span, :].astype(F32)
                     windows.append(window)
                     total = total + window * conv_ref[3 * row + col : 3 * row + col + 1, :]
             activ, slope = gelu_pair(total)
-            cot = cot_ref[cell, span, :]
+            cot = scale_ref[place, span, :]
             grad = (cot * conv_ref[9:10, :] * slope).astype(BF)
             pieces.append(grad)
             if own:
@@ -172,11 +170,11 @@
         grad_ref[cell] = grad
         return grad
 
-    one_cell(0, False)
-    one_cell(near - 1, False)
+    one_cell(0, False, edge_ref, 0)
+    one_cell(near - 1, False, edge_ref, 1)
 
     def own_cell(cell, carry):
-        grad = one_cell(cell + 1, True)
+        grad = one_cell(cell + 1, True, cot_ref, cell)
         turn_ref[:, cell, :] = jnp.dot(back, grad, preferred_element_type=F32)
         return carry
 
@@ -339,16 +337,15 @@
     sent, hidden, cotangent = tied(sent, hidden, cotangent)
     got = exchange(sent, "tile")
     head, tail = hidden[0, :2], hidden[0, cols - 2 :]
-    low_t = shifted(edge_pack(tail, split3(cotangent[0, cols - 1])), "tile", 1)
-    high_t = shifted(edge_pack(head, split3(cotangent[0, 0])), "tile", -1)
+    tail_cot = edge_pack(split3(cotangent[0, cols - 1]), bins)
+    head_cot = edge_pack(split3(cotangent[0, 0]), bins)
+    low_t = shifted(jnp.concatenate([tail_cot, tail], 0), "tile", 1)
+    high_t = shifted(jnp.concatenate([head, head_cot], 0), "tile", -1)
     far = [across(tail, 1), across(hidden[0], 0), across(head, -1)]
     got, low_t, high_t, far = tied(got, low_t, high_t, far)
     far = jnp.concatenate(far, 0)
-    low_cols, low_cot = edge_unpack(low_t)
-    high_cols, high_cot = edge_unpack(high_t)
-    wide = jnp.concatenate([low_cols, hidden[0], high_cols], 0)
-    cot_wide = jnp.concatenate([low_cot, cotangent[0], high_cot], 0)
-    cot_lanes = jnp.broadcast_to(cot_wide[:, :, None], (near, bins, chans))
+    wide = jnp.concatenate([low_t, hidden[0], high_t], 0)
+    cot_lanes = jnp.broadcast_to(cotangent[0][:, :, None], (cells, bins, chans))
     other = mate(got)
     close = mate(wide)
     grad_wide, grad_sent = on_core(
@@ -373,6 +370,7 @@
             pltpu.VMEM((16, 2 * modes, chans), F32),
             pltpu.VMEM((2 * modes, cells, chans), F32),
             pltpu.VMEM((count, 8, chans), F32),
+            pltpu.VMEM((2, bins, chans), F32),
         ],
     )
     far_grad = across(grad_wide, 0)

time: 123 us -> 123 us (level)
  waiting for transfers between devices: 33.7 us -> 35.3 us
    unnamed x22 -> x24, local copies, waits for them, and re-layouts: 3.43 us -> 4.17 us
  transfers between devices with their start and end apart: 12 -> 12, of which waited for: 4 -> 5; matrix products, arithmetic and copies ran while one was open for 2% -> 1% of each run, Pallas kernels for 4% -> 4%
where the time goes in v5:
time: 123 us; the launch traced here: 122 us
  starting transfers between devices  63.6 us (52%)
  waiting for transfers between devices  35.3 us (29%)
  Pallas kernels  13.1 us (11%)
  local copies, waits for them, and re-layouts  5.41 us (4%)
  other arithmetic  2.44 us (2%)
    all_to_all x3, starting transfers between devices, exchange(): return lax.all_to_all(value, axis, 0, 0, tiled=True)  37.7 us
    ppermute x4, waiting for transfers between devices, across(): return lax.ppermute(block, ('grp', 'tile'), pairs)  30.9 us
    pallas_call x4, Pallas kernels, on_core(): pl.pallas_call(kernel, out_shape=out_shape, in_specs=[pl.BlockSpec(memory...  13.1 us
    ppermute x4, starting transfers between devices, across(): return lax.ppermute(block, ('grp', 'tile'), pairs)  11.6 us
    ppermute x3, starting transfers between devices, mate(): lax.ppermute(block, 'grp', [(i, i ^ 1) for i in range(lax.axis_size('grp'...  8.7 us
    ppermute x2, starting transfers between devices, shifted(): return lax.ppermute(block, axis, pairs)  5.56 us
    unnamed x24, local copies, waits for them, and re-layouts  4.17 us
    all_to_all x3, waiting for transfers between devices, exchange(): return lax.all_to_all(value, axis, 0, 0, tiled=True)  3.8 us
  transfers between devices with their start and end apart: 12, of which 5 were waited for; matrix products, arithmetic and copies ran while one was open for 1% of the time, Pallas kernels for 4%

profile of v5, /device:TPU:1, one launch (start us, length us, event | category | flops | bytes accessed | tf_op | source)
XLA Modules:
  0.0 122.0 jit_solution(1550189318864117639)
XLA Ops:
  0.7 1.1 convolution_convert_fusion
  2.7 1.1 pad_maximum_fusion
  3.8 19.7 %all-to-all-start = ((bf16[64,72,128]{2,1,0:T(8,128)(2,1)}), bf16[64,72,128]{2,1,0:T(8,128)(2,1)S(1)}, u32[]{:S(2)}, u32[]{:S(2)}) async-start(bf16[64,72,128]{2,1,0:T(8,128)(2,1)} %pad_maximum_fusion), calls=%async_computation | async-start | bytes 2359296 | tf_op jit(solution)/shard_map/all_to_all | solution.py:74
  23.7 1.3 %collective-permute-start.1 = (bf16[3,128,128]{2,1,0:T(8,128)(2,1)S(1)}, bf16[3,128,128]{2,1,0:T(8,128)(2,1)S(1)}, u32[]{:S(2)}, u32[]{:S(2)}) collective-permute-start(bf16[3,128,128]{2,1,0:T(8,128)(2,1)S(1)} %pad_maximum_fusion.4), channel_id=1, source_target_pairs={{1,0},{2,1},{3,2},{4,3},{5,4},{6,5},{7,6},{8,7},{9,8},{10,9},{11,1... | collective-permute-start | bytes 294920 | tf_op jit(solution)/shard_map/ppermute | solution.py:16
  25.0 3.1 %collective-permute-start.3 = (bf16[8,128,128]{2,1,0:T(8,128)(2,1)S(1)}, bf16[8,128,128]{2,1,0:T(8,128)(2,1)}, u32[]{:S(2)}, u32[]{:S(2)}) collective-permute-start(bf16[8,128,128]{2,1,0:T(8,128)(2,1)S(1)} %bitcast.38), channel_id=1, source_target_pairs={{64,128},{65,129},{66,130},{67,131},{68,132},{69,133},{70,134},{71... | collective-permute-start | bytes 786440 | tf_op jit(solution)/shard_map/ppermute | solution.py:34
  28.2 4.3 %collective-permute-start = (bf16[3,128,128]{2,1,0:T(8,128)(2,1)S(1)}, bf16[3,128,128]{2,1,0:T(8,128)(2,1)S(1)}, u32[]{:S(2)}, u32[]{:S(2)}) collective-permute-start(bf16[3,128,128]{2,1,0:T(8,128)(2,1)S(1)} %pad_maximum_fusion.3), channel_id=1, source_target_pairs={{0,1},{1,2},{2,3},{3,4},{4,5},{5,6},{6,7},{7,8},{8,9},{9,10},{10,1... | collective-permute-start | bytes 294920 | tf_op jit(solution)/shard_map/ppermute | solution.py:16
  32.5 3.2 %collective-permute-start.2 = (bf16[2,128,128]{2,1,0:T(8,128)(2,1)S(1)}, bf16[2,128,128]{2,1,0:T(8,128)(2,1)S(1)}, u32[]{:S(2)}, u32[]{:S(2)}) collective-permute-start(bf16[2,128,128]{2,1,0:T(8,128)(2,1)S(1)} %get-tuple-element.43), channel_id=1, source_target_pairs={{64,129},{65,130},{66,131},{67,132},{68,133},{69,134},{70,135},{71... | collective-permute-start | bytes 196616 | tf_op jit(solution)/shard_map/ppermute | solution.py:34
  35.7 1.3 %collective-permute-start.4 = (bf16[2,128,128]{2,1,0:T(8,128)(2,1)S(1)}, bf16[2,128,128]{2,1,0:T(8,128)(2,1)}, u32[]{:S(2)}, u32[]{:S(2)}) collective-permute-start(bf16[2,128,128]{2,1,0:T(8,128)(2,1)S(1)} %get-tuple-element.42), channel_id=1, source_target_pairs={{65,128},{66,129},{67,130},{68,131},{69,132},{70,133},{71,134},{72... | collective-permute-start | bytes 196616 | tf_op jit(solution)/shard_map/ppermute | solution.py:34
  37.0 15.3 %collective-permute-done.2 = bf16[2,128,128]{2,1,0:T(8,128)(2,1)S(1)} collective-permute-done((bf16[2,128,128]{2,1,0:T(8,128)(2,1)S(1)}, bf16[2,128,128]{2,1,0:T(8,128)(2,1)S(1)}, u32[]{:S(2)}, u32[]{:S(2)}) %collective-permute-start.2) | collective-permute-done | bytes 65568 | tf_op jit(solution)/shard_map/ppermute | solution.py:34
  52.2 4.3 %collective-permute-done.4 = bf16[2,128,128]{2,1,0:T(8,128)(2,1)} collective-permute-done((bf16[2,128,128]{2,1,0:T(8,128)(2,1)S(1)}, bf16[2,128,128]{2,1,0:T(8,128)(2,1)}, u32[]{:S(2)}, u32[]{:S(2)}) %collective-permute-start.4) | collective-permute-done | bytes 65568 | tf_op jit(solution)/shard_map/ppermute | solution.py:34
  56.6 4.9 %collective-permute-start.5 = (bf16[64,72,128]{2,1,0:T(8,128)(2,1)S(1)}, bf16[64,72,128]{2,1,0:T(8,128)(2,1)S(1)}, u32[]{:S(2)}, u32[]{:S(2)}) collective-permute-start(bf16[64,72,128]{2,1,0:T(8,128)(2,1)S(1)} %all-to-all-done.got_ref), channel_id=1, source_target_pairs={{0,64},{64,0},{128,192},{192,128},{256,320},{320,256},{384,448},{4... | collective-permute-start | bytes 3538952 | tf_op jit(solution)/shard_map/ppermute | solution.py:20
  61.5 1.9 %collective-permute-start.6 = (bf16[14,128,128]{2,1,0:T(8,128)(2,1)S(1)}, bf16[14,128,128]{2,1,0:T(8,128)(2,1)S(1)}, u32[]{:S(2)}, u32[]{:S(2)}) collective-permute-start(bf16[14,128,128]{2,1,0:T(8,128)(2,1)S(1)} %pad_maximum_fusion.1.wide_ref), channel_id=1, source_target_pairs={{0,64},{64,0},{128,192},{192,128},{256,320},{320,256},{384,448},{4... | collective-permute-start | bytes 1376264 | tf_op jit(solution)/shard_map/ppermute | solution.py:20
  63.6 1.0 pad_maximum_fusion.2.far_ref
  65.5 6.1 %shard_map.93 = (bf16[10,128,128]{2,1,0:T(8,128)(2,1)S(1)}, bf16[64,32,128]{2,1,0:T(8,128)(2,1)}) custom-call(s32[1]{0:T(128)} %bitcast.core_ref, bf16[64,72,128]{2,1,0:T(8,128)(2,1)S(1)} %all-to-all-done.got_ref, bf16[64,72,128]{2,1,0:T(8,128)(2,1)S(1)} %collective-permute-done.5.other_ref, bf16[12,128,128]{2,1,0:T(8,128)(2,1)S(1)} %pad_maximum_fusion.2.far_ref, ...), custom_call_target="tpu_custom_call" | custom-call | flops 200000000 | bytes 12000000 | tf_op jit(solution)/shard_map/pallas_call | solution.py:289
  72.3 9.6 %all-to-all-start.1 = ((bf16[64,32,128]{2,1,0:T(8,128)(2,1)}), bf16[64,32,128]{2,1,0:T(8,128)(2,1)S(1)}, u32[]{:S(2)}, u32[]{:S(2)}) async-start(bf16[64,32,128]{2,1,0:T(8,128)(2,1)} %get-tuple-element.31.sent_ref), calls=%async_computation.1 | async-start | bytes 1048576 | tf_op jit(solution)/shard_map/all_to_all | solution.py:74
  82.0 4.0 %collective-permute-start.7 = (bf16[10,128,128]{2,1,0:T(8,128)(2,1)}, bf16[10,128,128]{2,1,0:T(8,128)(2,1)S(1)}, u32[]{:S(2)}, u32[]{:S(2)}) collective-permute-start(bf16[10,128,128]{2,1,0:T(8,128)(2,1)} %copy-done), channel_id=1, source_target_pairs={{64,128},{65,129},{66,130},{67,131},{68,132},{69,133},{70,134},{71... | collective-permute-start | bytes 983048 | tf_op jit(solution)/shard_map/ppermute | solution.py:34
  86.0 1.9 %collective-permute-start.8 = (bf16[10,128,128]{2,1,0:T(8,128)(2,1)}, bf16[10,128,128]{2,1,0:T(8,128)(2,1)S(1)}, u32[]{:S(2)}, u32[]{:S(2)}) collective-permute-start(bf16[10,128,128]{2,1,0:T(8,128)(2,1)} %copy-done), channel_id=1, source_target_pairs={{0,64},{64,0},{128,192},{192,128},{256,320},{320,256},{384,448},{4... | collective-permute-start | bytes 983048 | tf_op jit(solution)/shard_map/ppermute | solution.py:20
  88.2 11.3 %collective-permute-done.7.far_ref = bf16[10,128,128]{2,1,0:T(8,128)(2,1)S(1)} collective-permute-done((bf16[10,128,128]{2,1,0:T(8,128)(2,1)}, bf16[10,128,128]{2,1,0:T(8,128)(2,1)S(1)}, u32[]{:S(2)}, u32[]{:S(2)}) %collective-permute-start.7) | collective-permute-done | bytes 327712 | tf_op jit(solution)/shard_map/ppermute | solution.py:34
  100.9 1.0 shard_map.95
  102.0 8.4 %all-to-all-start.2 = ((bf16[8,176,128]{2,1,0:T(8,128)(2,1)}), bf16[8,176,128]{2,1,0:T(8,128)(2,1)S(1)}, u32[]{:S(2)}, u32[]{:S(2)}) async-start(bf16[8,176,128]{2,1,0:T(8,128)(2,1)} %shard_map.95), calls=%async_computation.2 | async-start | bytes 720896 | tf_op jit(solution)/shard_map/all_to_all | solution.py:74
  110.3 1.0 copy-done.3
  111.3 1.0 copy-done.5
  112.3 5.2 %shard_map.94 = f32[8,128,128]{2,1,0:T(8,128)} custom-call(s32[1]{0:T(128)} %bitcast.core_ref, bf16[64,72,128]{2,1,0:T(8,128)(2,1)S(1)} %all-to-all-done.got_ref, bf16[64,72,128]{2,1,0:T(8,128)(2,1)S(1)} %collective-permute-done.5.other_ref, bf16[64,32,128]{2,1,0:T(8,128)(2,1)} %get-tuple-element.31.sent_ref, bf16[10,128,128]{2,1,0:T(8,128)(2,1)S(1)} %copy-done.3, ...), custom_call_target="tpu_custom_call" | custom-call | flops 200000000 | bytes 12000000 | tf_op jit(solution)/shard_map/pallas_call | solution.py:289
  117.5 3.8 %all-to-all-done.2.last_ref = bf16[8,176,128]{2,1,0:T(8,128)(2,1)S(1)} async-done(((bf16[8,176,128]{2,1,0:T(8,128)(2,1)}), bf16[8,176,128]{2,1,0:T(8,128)(2,1)S(1)}, u32[]{:S(2)}, u32[]{:S(2)}) %all-to-all-start.2) | async-done | bytes 360480 | tf_op jit(solution)/shard_map/all_to_all | solution.py:74
  (52 shorter events, 5.0 us)
Async XLA Ops:
  0.6 1.8 %copy-start.8 = (bf16[64,256]{1,0:T(8,128)(2,1)S(1)}, bf16[64,256]{1,0:T(8,128)(2,1)}, u32[]{:S(2)}) copy-start(bf16[64,256]{1,0:T(8,128)(2,1)} %param.8) | copy-start | bytes 98308
  3.8 19.7 %copy-start.9 = (f32[1,8,128]{2,1,0:T(8,128)S(1)}, f32[1,8,128]{2,1,0:T(8,128)}, u32[]{:S(2)}) copy-start(f32[1,8,128]{2,1,0:T(8,128)} %param.7) | copy-start | bytes 12292
  3.8 19.8 %copy-start.7 = (bf16[1,8,128,128]{3,2,1,0:T(8,128)(2,1)S(1)}, bf16[1,8,128,128]{3,2,1,0:T(8,128)(2,1)}, u32[]{:S(2)}) copy-start(bf16[1,8,128,128]{3,2,1,0:T(8,128)(2,1)} %param.6) | copy-start | bytes 786436
  3.8 52.8 %all-to-all-start = ((bf16[64,72,128]{2,1,0:T(8,128)(2,1)}), bf16[64,72,128]{2,1,0:T(8,128)(2,1)S(1)}, u32[]{:S(2)}, u32[]{:S(2)}) async-start(bf16[64,72,128]{2,1,0:T(8,128)(2,1)} %pad_maximum_fusion), calls=%async_computation | async-start | bytes 2359296 | tf_op jit(solution)/shard_map/all_to_all | solution.py:74
  23.6 39.9 %copy-start.10 = (f32[9,128]{1,0:T(8,128)S(1)}, f32[9,128]{1,0:T(8,128)}, u32[]{:S(2)}) copy-start(f32[9,128]{1,0:T(8,128)} %param.9) | copy-start | bytes 13828
  23.6 39.9 %copy-start.11 = (f32[128]{0:T(128)S(1)}, f32[128]{0:T(128)}, u32[]{:S(2)}) copy-start(f32[128]{0:T(128)} %param.10) | copy-start | bytes 1540
  23.7 32.9 %collective-permute-start.1 = (bf16[3,128,128]{2,1,0:T(8,128)(2,1)S(1)}, bf16[3,128,128]{2,1,0:T(8,128)(2,1)S(1)}, u32[]{:S(2)}, u32[]{:S(2)}) collective-permute-start(bf16[3,128,128]{2,1,0:T(8,128)(2,1)S(1)} %pad_maximum_fusion.4), channel_id=1, source_target_pairs={{1,0},{2,1},{3,2},{4,3},{5,4},{6,5},{7,6},{8,7},{9,8},{10,9},{11,1... | collective-permute-start | bytes 294920 | tf_op jit(solution)/shard_map/ppermute | solution.py:16
  25.0 31.6 %collective-permute-start.3 = (bf16[8,128,128]{2,1,0:T(8,128)(2,1)S(1)}, bf16[8,128,128]{2,1,0:T(8,128)(2,1)}, u32[]{:S(2)}, u32[]{:S(2)}) collective-permute-start(bf16[8,128,128]{2,1,0:T(8,128)(2,1)S(1)} %bitcast.38), channel_id=1, source_target_pairs={{64,128},{65,129},{66,130},{67,131},{68,132},{69,133},{70,134},{71... | collective-permute-start | bytes 786440 | tf_op jit(solution)/shard_map/ppermute | solution.py:34
  28.2 37.3 %copy-start.6 = (bf16[128,128]{1,0:T(8,128)(2,1)S(1)}, bf16[128,128]{1,0:T(8,128)(2,1)}, u32[]{:S(2)}) copy-start(bf16[128,128]{1,0:T(8,128)(2,1)} %constant.31.clone.table_ref) | copy-start | bytes 98308
  28.2 28.4 %collective-permute-start = (bf16[3,128,128]{2,1,0:T(8,128)(2,1)S(1)}, bf16[3,128,128]{2,1,0:T(8,128)(2,1)S(1)}, u32[]{:S(2)}, u32[]{:S(2)}) collective-permute-start(bf16[3,128,128]{2,1,0:T(8,128)(2,1)S(1)} %pad_maximum_fusion.3), channel_id=1, source_target_pairs={{0,1},{1,2},{2,3},{3,4},{4,5},{5,6},{6,7},{7,8},{8,9},{9,10},{10,1... | collective-permute-start | bytes 294920 | tf_op jit(solution)/shard_map/ppermute | solution.py:16
  32.5 19.8 %collective-permute-start.2 = (bf16[2,128,128]{2,1,0:T(8,128)(2,1)S(1)}, bf16[2,128,128]{2,1,0:T(8,128)(2,1)S(1)}, u32[]{:S(2)}, u32[]{:S(2)}) collective-permute-start(bf16[2,128,128]{2,1,0:T(8,128)(2,1)S(1)} %get-tuple-element.43), channel_id=1, source_target_pairs={{64,129},{65,130},{66,131},{67,132},{68,133},{69,134},{70,135},{71... | collective-permute-start | bytes 196616 | tf_op jit(solution)/shard_map/ppermute | solution.py:34
  35.7 20.9 %collective-permute-start.4 = (bf16[2,128,128]{2,1,0:T(8,128)(2,1)S(1)}, bf16[2,128,128]{2,1,0:T(8,128)(2,1)}, u32[]{:S(2)}, u32[]{:S(2)}) collective-permute-start(bf16[2,128,128]{2,1,0:T(8,128)(2,1)S(1)} %get-tuple-element.42), channel_id=1, source_target_pairs={{65,128},{66,129},{67,130},{68,131},{69,132},{70,133},{71,134},{72... | collective-permute-start | bytes 196616 | tf_op jit(solution)/shard_map/ppermute | solution.py:34
  56.6 8.7 %collective-permute-start.5 = (bf16[64,72,128]{2,1,0:T(8,128)(2,1)S(1)}, bf16[64,72,128]{2,1,0:T(8,128)(2,1)S(1)}, u32[]{:S(2)}, u32[]{:S(2)}) collective-permute-start(bf16[64,72,128]{2,1,0:T(8,128)(2,1)S(1)} %all-to-all-done.got_ref), channel_id=1, source_target_pairs={{0,64},{64,0},{128,192},{192,128},{256,320},{320,256},{384,448},{4... | collective-permute-start | bytes 3538952 | tf_op jit(solution)/shard_map/ppermute | solution.py:20
  61.5 3.7 %collective-permute-start.6 = (bf16[14,128,128]{2,1,0:T(8,128)(2,1)S(1)}, bf16[14,128,128]{2,1,0:T(8,128)(2,1)S(1)}, u32[]{:S(2)}, u32[]{:S(2)}) collective-permute-start(bf16[14,128,128]{2,1,0:T(8,128)(2,1)S(1)} %pad_maximum_fusion.1.wide_ref), channel_id=1, source_target_pairs={{0,64},{64,0},{128,192},{192,128},{256,320},{320,256},{384,448},{4... | collective-permute-start | bytes 1376264 | tf_op jit(solution)/shard_map/ppermute | solution.py:20
  71.6 0.7 copy-start
  72.3 28.6 %all-to-all-start.1 = ((bf16[64,32,128]{2,1,0:T(8,128)(2,1)}), bf16[64,32,128]{2,1,0:T(8,128)(2,1)S(1)}, u32[]{:S(2)}, u32[]{:S(2)}) async-start(bf16[64,32,128]{2,1,0:T(8,128)(2,1)} %get-tuple-element.31.sent_ref), calls=%async_computation.1 | async-start | bytes 1048576 | tf_op jit(solution)/shard_map/all_to_all | solution.py:74
  82.0 17.5 %collective-permute-start.7 = (bf16[10,128,128]{2,1,0:T(8,128)(2,1)}, bf16[10,128,128]{2,1,0:T(8,128)(2,1)S(1)}, u32[]{:S(2)}, u32[]{:S(2)}) collective-permute-start(bf16[10,128,128]{2,1,0:T(8,128)(2,1)} %copy-done), channel_id=1, source_target_pairs={{64,128},{65,129},{66,130},{67,131},{68,132},{69,133},{70,134},{71... | collective-permute-start | bytes 983048 | tf_op jit(solution)/shard_map/ppermute | solution.py:34
  86.0 14.2 %collective-permute-start.8 = (bf16[10,128,128]{2,1,0:T(8,128)(2,1)}, bf16[10,128,128]{2,1,0:T(8,128)(2,1)S(1)}, u32[]{:S(2)}, u32[]{:S(2)}) collective-permute-start(bf16[10,128,128]{2,1,0:T(8,128)(2,1)} %copy-done), channel_id=1, source_target_pairs={{0,64},{64,0},{128,192},{192,128},{256,320},{320,256},{384,448},{4... | collective-permute-start | bytes 983048 | tf_op jit(solution)/shard_map/ppermute | solution.py:20
  88.1 22.3 %copy-start.1 = (bf16[10,128,128]{2,1,0:T(8,128)(2,1)S(1)}, bf16[10,128,128]{2,1,0:T(8,128)(2,1)}, u32[]{:S(2)}) copy-start(bf16[10,128,128]{2,1,0:T(8,128)(2,1)} %copy-done) | copy-start | bytes 983044
  99.5 0.7 copy-start.2
  100.2 0.7 copy-start.4
  102.0 19.4 %all-to-all-start.2 = ((bf16[8,176,128]{2,1,0:T(8,128)(2,1)}), bf16[8,176,128]{2,1,0:T(8,128)(2,1)S(1)}, u32[]{:S(2)}, u32[]{:S(2)}) async-start(bf16[8,176,128]{2,1,0:T(8,128)(2,1)} %shard_map.95), calls=%async_computation.2 | async-start | bytes 720896 | tf_op jit(solution)/shard_map/all_to_all | solution.py:74
  110.3 1.0 copy-start.3
  111.3 1.0 copy-start.5
